TPU v7x, 32 devices: a whole 2x2x4 slice. The times are simulated.
32 devices in a mesh: ctx: 8 (over z, y), head: 4 (over x, core).
Axes of the slice: x: 2, y: 2, z: 4, core: 2. Of those that a mesh axis runs over, the one named last changes fastest.
Arguments:
- query: bfloat16 [8, 2, 512, 4096], P('ctx', None, None, 'head'), may hold values from -48 to 48
- key: bfloat16 [8, 2, 512, 512], P('ctx', None, 'head'), may hold values from -18 to 18
- value: bfloat16 [8, 2, 512, 512], P('ctx', None, 'head'), may hold values from -6 to 6
- d_out: bfloat16 [8, 2, 512, 4096], P('ctx', None, None, 'head'), may hold values from -6 to 6
- doc_start: int32 [64], replicated, may hold values from 0 to 1, as said below
Outputs:
- d_query: bfloat16 [8, 2, 512, 4096], P('ctx', None, None, 'head')
- d_key: bfloat16 [8, 2, 512, 512], P('ctx', None, 'head')
- d_value: bfloat16 [8, 2, 512, 512], P('ctx', None, 'head')
Inputs may be any that keep to these rules, and one draw needn't show every extreme that they name: `doc_start`: 1 where a document begins at that block of 128 tokens (blocks in sequence order); block 0 begins one; from every beginning the next beginning, or the end of the sequence, is 1 to 3 blocks away; the first block of every span after the first lies inside a document of exactly 3 blocks that began in the span before.
All inputs are finite; a program needn't handle non-finite values.
Results may differ from a plain program's by a relative error of at most 0.039.
Values may be sent and summed in bfloat16 or wider, within the bound.
No kernel may reach another device: no remote copies, remote signals or barrier semaphores. Data moves between devices by JAX's collectives and lax.ppermute only.
A program may use at most 64 MiB of HBM per device.

v0:
```python
import jax
import jax.numpy as jnp
from jax import lax
from jax.sharding import PartitionSpec as P

HD = 128
BLK = 128
GROUP = 8


def padded_2(cells, sides, width):
    for axis, dim in sides:
        count = lax.axis_size(axis)
        ends = count - 1
        head = lax.slice_in_dim(cells, 0, width, axis=dim)
        tail = lax.slice_in_dim(cells, cells.shape[dim] - width, cells.shape[dim], axis=dim)
        cells = jnp.concatenate(
            [
                lax.ppermute(tail, axis, [(i, (i + 1) % count) for i in range(ends)]),
                cells,
                lax.ppermute(head, axis, [((i + 1) % count, i) for i in range(ends)]),
            ],
            axis=dim,
        )
    return cells


def windowed(extended, reach_rows, blocks):
    pieces = []
    for offset in range(reach_rows // BLK + 1):
        sliced = lax.slice_in_dim(extended, offset * BLK, offset * BLK + blocks * BLK, axis=0)
        pieces.append(sliced.reshape((blocks, BLK) + extended.shape[1:]))
    return jnp.concatenate(pieces, axis=1)


def unwindowed(windows, reach_rows, blocks):
    summed = None
    for offset in range(reach_rows // BLK + 1):
        sliced = windows[:, offset * BLK : (offset + 1) * BLK].reshape(
            (blocks * BLK,) + windows.shape[2:]
        )
        padded = jnp.pad(
            sliced, ((offset * BLK, reach_rows - offset * BLK),) + ((0, 0),) * (windows.ndim - 2)
        )
        summed = padded if summed is None else summed + padded
    return summed


def span_grads(queries, grads_out, keys_ext, values_ext, doc_begins, span_start, reach_rows):
    blocks = queries.shape[0] // BLK
    kv_heads = keys_ext.shape[1] // HD
    score_scale = HD ** (-0.5)
    q_blocks = queries.reshape(blocks, BLK, kv_heads, GROUP, HD)
    do_blocks = grads_out.reshape(blocks, BLK, kv_heads, GROUP, HD)
    k_windows = windowed(keys_ext.reshape(-1, kv_heads, HD), reach_rows, blocks)
    v_windows = windowed(values_ext.reshape(-1, kv_heads, HD), reach_rows, blocks)
    row_pos = jnp.arange(BLK, dtype=jnp.int32)[None, :, None]
    col_pos = jnp.arange(reach_rows + BLK, dtype=jnp.int32)[None, None, :]
    key_pos = (
        span_start - reach_rows + jnp.arange(blocks, dtype=jnp.int32)[:, None, None] * BLK + col_pos
    )
    visible = (col_pos <= row_pos + reach_rows) & (key_pos >= doc_begins[:, None, None])
    visible = visible[:, None, None]
    scores = (
        jnp.einsum("btgjd,bkgd->bgjtk", q_blocks, k_windows, preferred_element_type=jnp.float32)
        * score_scale
    )
    peak = jnp.max(jnp.where(visible, scores, -1e30), axis=-1, keepdims=True)
    weights = jnp.exp(jnp.where(visible, scores - peak, -1e30))
    probs = weights / jnp.sum(weights, axis=-1, keepdims=True)
    probs_b = probs.astype(jnp.bfloat16)
    outputs = jnp.einsum(
        "bgjtk,bkgd->btgjd", probs_b, v_windows, preferred_element_type=jnp.float32
    ).astype(jnp.bfloat16)
    deltas = jnp.sum(do_blocks.astype(jnp.float32) * outputs.astype(jnp.float32), axis=-1)
    dprobs = jnp.einsum(
        "btgjd,bkgd->bgjtk", do_blocks, v_windows, preferred_element_type=jnp.float32
    )
    dscores = (
        probs * (dprobs - jnp.transpose(deltas, (0, 2, 3, 1))[..., None]) * score_scale
    ).astype(jnp.bfloat16)
    d_queries = jnp.einsum(
        "bgjtk,bkgd->btgjd", dscores, k_windows, preferred_element_type=jnp.float32
    ).astype(jnp.bfloat16)
    dk_windows = jnp.einsum(
        "bgjtk,btgjd->bkgd", dscores, q_blocks, preferred_element_type=jnp.float32
    )
    dv_windows = jnp.einsum(
        "bgjtk,btgjd->bkgd", probs_b, do_blocks, preferred_element_type=jnp.float32
    )
    return (
        d_queries.reshape(blocks * BLK, -1),
        unwindowed(dk_windows, reach_rows, blocks).reshape(-1, kv_heads * HD),
        unwindowed(dv_windows, reach_rows, blocks).reshape(-1, kv_heads * HD),
    )


def per_device(query, key, value, d_out, doc_start):
    kv_key, kv_value = (
        lax.all_to_all(key, "head", split_axis=3, concat_axis=2, tiled=True),
        lax.all_to_all(value, "head", split_axis=3, concat_axis=2, tiled=True),
    )
    span_rows = kv_key.shape[2]
    ctx_index = lax.axis_index("ctx")
    ctx_count = lax.axis_size("ctx")
    is_last = ctx_index == ctx_count - 1
    rim_from = span_rows - span_rows
    outgoing = jnp.stack(
        [
            jnp.stack([kv_key[0, 1, rim_from:], kv_value[0, 1, rim_from:]]),
            jnp.stack([kv_key[0, 0, rim_from:], kv_value[0, 0, rim_from:]]),
        ]
    )
    incoming = padded_2(outgoing, (("ctx", 0),), 1)
    previous = [incoming[0], jnp.where(is_last, outgoing[1], incoming[3])]
    run_begin = (
        lax.cummax(
            jnp.where(doc_start == 1, jnp.arange(doc_start.shape[0], dtype=jnp.int32), 0), axis=0
        )
        * BLK
    )
    blocks = span_rows // BLK
    span_results = []
    for span_slot in range(2):
        span_id = ctx_index if span_slot == 0 else 2 * ctx_count - 1 - ctx_index
        span_start = span_id * span_rows
        doc_begins = lax.dynamic_slice_in_dim(run_begin, span_id * blocks, blocks)
        keys_ext = jnp.concatenate([previous[span_slot][0], kv_key[0, span_slot]], axis=0)
        values_ext = jnp.concatenate([previous[span_slot][1], kv_value[0, span_slot]], axis=0)
        span_results.append(
            span_grads(
                query[0, span_slot],
                d_out[0, span_slot],
                keys_ext,
                values_ext,
                doc_begins,
                span_start,
                span_rows,
            )
        )
    partials = jnp.stack(
        [
            jnp.stack([span_results[0][1][:span_rows], span_results[0][2][:span_rows]]),
            jnp.stack([span_results[1][1][:span_rows], span_results[1][2][:span_rows]]),
        ]
    )
    returned = padded_2(partials.astype(jnp.bfloat16), (("ctx", 0),), 1).astype(partials.dtype)
    added_parts = [returned[3] + jnp.where(is_last, partials[1], 0.0), returned[0]]
    key_grads = []
    value_grads = []
    for span_slot in range(2):
        own_key = (
            span_results[span_slot][1][span_rows:].at[rim_from:].add(added_parts[span_slot][0])
        )
        own_value = (
            span_results[span_slot][2][span_rows:].at[rim_from:].add(added_parts[span_slot][1])
        )
        key_grads.append(own_key.astype(jnp.bfloat16))
        value_grads.append(own_value.astype(jnp.bfloat16))
    d_query = jnp.stack([span_results[0][0], span_results[1][0]])[None]
    key_layout = jnp.stack(key_grads)[None]
    value_layout = jnp.stack(value_grads)[None]
    d_key, d_value = (
        lax.all_to_all(key_layout, "head", split_axis=2, concat_axis=3, tiled=True),
        lax.all_to_all(value_layout, "head", split_axis=2, concat_axis=3, tiled=True),
    )
    return (d_query, d_key, d_value)


def solution(mesh):
    return jax.shard_map(
        per_device,
        mesh=mesh,
        in_specs=(
            P("ctx", None, None, "head"),
            P("ctx", None, "head", None),
            P("ctx", None, "head", None),
            P("ctx", None, None, "head"),
            P(),
        ),
        out_specs=(
            P("ctx", None, None, "head"),
            P("ctx", None, "head", None),
            P("ctx", None, "head", None),
        ),
        check_vma=False,
    )
```

profile of v0, /device:TPU:0, one launch (start us, length us, event | category | flops | bytes accessed | tf_op | source)
XLA Modules:
  0.0 138.9 jit_solution(7004129556165179096)
XLA Ops:
  0.6 1.8 %copy.46 = bf16[1,2,128,512]{2,1,0,3:T(2,128)(2,1)} copy(bf16[1,2,128,512]{3,2,1,0:T(8,128)(2,1)} %param.22) | data formatting | bytes 524288 | tf_op args[1]
  2.5 4.2 %all-to-all-start = ((bf16[1,2,128,512]{2,1,0,3:T(2,128)(2,1)}), bf16[1,2,128,512]{2,1,0,3:T(2,128)(2,1)S(1)}, u32[]{:S(2)}, u32[]{:S(2)}) async-start(bf16[1,2,128,512]{2,1,0,3:T(2,128)(2,1)} %copy.46), calls=%async_computation | async-start | bytes 524288 | tf_op jit(solution)/shard_map/all_to_all | solution.py:100
  6.7 0.7 fusion.92
  7.5 1.8 %copy.48 = bf16[1,2,128,512]{2,1,0,3:T(2,128)(2,1)} copy(bf16[1,2,128,512]{3,2,1,0:T(8,128)(2,1)} %param.23) | data formatting | bytes 524288 | tf_op args[2]
  9.4 1.7 %slice_bitcast_fusion.1 = (bf16[64,8,8,128]{3,1,2,0:T(8,128)(2,1)S(1)}, bf16[64,8,8,128]{3,1,2,0:T(8,128)(2,1)S(1)}) fusion(bf16[1,2,512,1024]{3,2,1,0:T(8,128)(2,1)} %param.21), kind=kLoop, calls=%fused_computation.56 | loop fusion | bytes 4194304
  11.1 4.6 %slice_bitcast_fusion.3 = (bf16[64,8,8,128]{3,1,2,0:T(8,128)(2,1)}, f32[64,8,8,128]{3,1,2,0:T(8,128)}, f32[64,8,8,128]{3,1,2,0:T(8,128)}, bf16[64,8,8,128]{3,1,2,0:T(8,128)(2,1)}) fusion(bf16[1,2,512,1024]{3,2,1,0:T(8,128)(2,1)} %param.24), kind=kLoop, calls=%fused_computation.68 | loop fusion | flops 1048576 | bytes 8388608
  15.9 3.4 %all-to-all-start.1 = ((bf16[1,2,128,512]{2,1,0,3:T(2,128)(2,1)}), bf16[1,2,128,512]{2,1,0,3:T(2,128)(2,1)S(1)}, u32[]{:S(2)}, u32[]{:S(2)}) async-start(bf16[1,2,128,512]{2,1,0,3:T(2,128)(2,1)} %copy.48), calls=%async_computation.1 | async-start | bytes 524288 | tf_op jit(solution)/shard_map/all_to_all | solution.py:101
  19.3 0.7 iota_compare_fusion
  20.2 5.2 %all-to-all-done.1 = bf16[1,2,128,512]{2,1,0,3:T(2,128)(2,1)S(1)} async-done(((bf16[1,2,128,512]{2,1,0,3:T(2,128)(2,1)}), bf16[1,2,128,512]{2,1,0,3:T(2,128)(2,1)S(1)}, u32[]{:S(2)}, u32[]{:S(2)}) %all-to-all-start.1) | async-done | bytes 262176 | tf_op jit(solution)/shard_map/all_to_all | solution.py:101
  25.4 0.2 copy.49
  25.6 1.0 fusion.103
  26.6 0.7 maximum_bitcast_fusion.1
  27.3 1.3 collective-permute-start.1
  28.7 0.3 copy.100
  28.9 0.3 copy.103
  29.2 2.5 %copy.101 = bf16[64,8,8,128]{3,2,1,0:T(8,128)(2,1)} copy(bf16[64,8,8,128]{3,1,2,0:T(8,128)(2,1)} %get-tuple-element.85) | data formatting | bytes 2097152
  31.7 1.5 %copy.104 = bf16[64,8,8,128]{3,2,1,0:T(8,128)(2,1)S(1)} copy(bf16[64,8,8,128]{3,1,2,0:T(8,128)(2,1)} %get-tuple-element.88) | data formatting | bytes 2097152
  33.2 3.4 %copy.102 = f32[64,8,8,128]{3,2,1,0:T(8,128)} copy(f32[64,8,8,128]{3,1,2,0:T(8,128)} %get-tuple-element.86) | data formatting | bytes 4194304
  36.6 2.9 %copy.55 = f32[4,128,1,8,128]{1,4,3,0,2:T(8,128)} copy(f32[4,128,1,8,128]{4,3,2,1,0:T(8,128)} %bitcast.412) | data formatting | bytes 4194304 | tf_op jit(solution)/shard_map/convert_element_type | solution.py:75
  39.5 3.4 %copy.105 = f32[64,8,8,128]{3,2,1,0:T(8,128)} copy(f32[64,8,8,128]{3,1,2,0:T(8,128)} %get-tuple-element.87) | data formatting | bytes 4194304
  42.9 2.9 %copy.63 = f32[4,128,1,8,128]{1,4,3,0,2:T(8,128)} copy(f32[4,128,1,8,128]{4,3,2,1,0:T(8,128)} %bitcast.413) | data formatting | bytes 4194304 | tf_op jit(solution)/shard_map/convert_element_type | solution.py:75
  45.8 2.2 %broadcast_and_fusion.1 = (pred[4,128,640]{1,2,0:T(8,128)(4,1)S(1)}, pred[4,128,640]{1,2,0:T(8,128)(4,1)S(1)}) fusion(pred[4,640]{1,0:T(4,128)(4,1)S(1)} %get-tuple-element.162, pred[128,640]{0,1:T(8,128)(4,1)} %iota_compare_fusion, pred[4,640]{1,0:T(4,128)(4,1)S(1)} %get-tuple-element.161), kind=kLoop, calls=%fused_computation.78 | loop fusion | flops 655360 | bytes 742400 | tf_op jit(solution)/shard_map/and | solution.py:62
  48.0 1.8 %fusion.81 = (bf16[1,2,512,128]{3,2,1,0:T(8,128)(2,1)}, bf16[2,512,128]{2,1,0:T(8,128)(2,1)S(1)}) fusion(bf16[1,512,128]{2,1,0:T(8,128)(2,1)} %get-tuple-element.159, bf16[1,512,128]{2,1,0:T(8,128)(2,1)} %get-tuple-element.116, bf16[1,2,512,128]{3,2,1,0:T(8,128)(2,1)} %collective-permute-done.1, pred[]{:T(512)S(6)} %eq.11), kind=kLoop, calls=%fused_computation.125 | loop fusion | flops 262144 | bytes 1048577 | tf_op jit(solution)/shard_map/stack | solution.py:108
  49.8 5.4 %collective-permute-start = (bf16[1,2,512,128]{3,2,1,0:T(8,128)(2,1)}, bf16[1,2,512,128]{3,2,1,0:T(8,128)(2,1)}, u32[]{:S(2)}, u32[]{:S(2)}) collective-permute-start(bf16[1,2,512,128]{3,2,1,0:T(8,128)(2,1)} %get-tuple-element.137), channel_id=1, source_target_pairs={{0,4},{4,8},{8,12},{12,16},{16,20},{20,24},{24,28},{1,5},{5,9},{9,... | collective-permute-start | bytes 786440 | tf_op jit(solution)/shard_map/ppermute | solution.py:19
  55.5 0.9 constant_dynamic-update-slice_fusion.15
  56.5 1.6 %fusion.6 = (f32[4,8,128]{2,1,0:T(8,128)S(1)}, f32[4,640,128,8]{2,1,3,0:T(8,128)S(1)}) fusion(pred[4,128,640]{1,2,0:T(8,128)(4,1)S(1)} %get-tuple-element.150, bf16[4,128,8,128]{3,2,1,0:T(8,128)(2,1)S(1)} %bitcast.410, bf16[4,640,1,128]{3,1,0,2:T(8,128)(2,1)S(1)} %constant_dynamic-update-slice_fusion.10), kind=kOutput, calls=%fused_computation.10 | convolution fusion | flops 678948864 | bytes 12533760 | tf_op jit(solution)/shard_map/btgjd,bkgd->bgjtk/dot_general | solution.py:65
  58.2 2.4 %fusion.15 = f32[4,8,128]{2,1,0:T(8,128)S(1)} fusion(f32[4,640,128,8]{2,1,3,0:T(8,128)S(1)} %get-tuple-element.152, f32[4,8,128]{2,1,0:T(8,128)S(1)} %get-tuple-element.151, pred[4,128,640]{1,2,0:T(8,128)(4,1)S(1)} %get-tuple-element.150), kind=kLoop, calls=%fused_computation.21 | loop fusion | flops 10481664 | bytes 10846208 | tf_op jit(solution)/shard_map/reduce_sum | solution.py:70
  60.6 3.1 %fusion.41 = f32[4,640,1,128]{3,1,0,2:T(8,128)S(1)} fusion(bf16[4,128,8,128]{3,2,1,0:T(8,128)(2,1)S(1)} %bitcast.437, f32[4,8,128]{2,1,0:T(8,128)S(1)} %fusion.15, f32[4,8,128]{2,1,0:T(8,128)S(1)} %get-tuple-element.151, f32[4,640,128,8]{2,1,3,0:T(8,128)S(1)} %get-tuple-element.152, pred[4,128,640]{1,2,0:T(8,128)(4,1)S(1)} %get-tuple-element.150), kind=kOutput, calls=%fused_computation.50 | convolution fusion | flops 684195840 | bytes 13205504 | tf_op jit(solution)/shard_map/bgjtk,btgjd->bkgd/dot_general | solution.py:88
  63.7 3.2 %fusion.29 = f32[4,128,8]{1,2,0:T(8,128)S(1)} fusion(f32[4,128,1,8,128]{1,4,3,0,2:T(8,128)S(1)} %copy-done.6, bf16[4,640,1,128]{3,1,0,2:T(8,128)(2,1)S(1)} %constant_dynamic-update-slice_fusion.15, f32[4,8,128]{2,1,0:T(8,128)S(1)} %fusion.15, f32[4,8,128]{2,1,0:T(8,128)S(1)} %get-tuple-element.151, f32[4,640,128,8]{2,1,3,0:T(8,128)S(1)} %get-tuple-element.152, ...), kind=kOutput, calls=%fused_computation.37 | convolution fusion | flops 686288896 | bytes 13615104 | tf_op jit(solution)/shard_map/bgjtk,bkgd->btgjd/dot_general | solution.py:72
  66.9 4.2 %fusion.17 = bf16[4,8,128,640]{2,3,1,0:T(8,128)(2,1)S(1)} fusion(f32[4,8,128]{2,1,0:T(8,128)S(1)} %bitcast.466, f32[4,8,128]{2,1,0:T(8,128)S(1)} %fusion.15, f32[4,8,128]{2,1,0:T(8,128)S(1)} %get-tuple-element.151, f32[4,640,128,8]{2,1,3,0:T(8,128)S(1)} %get-tuple-element.152, pred[4,128,640]{1,2,0:T(8,128)(4,1)S(1)} %get-tuple-element.150, ...), kind=kOutput, calls=%fused_computation.23 | convolution fusion | flops 692060160 | bytes 17809408 | tf_op jit(solution)/shard_map/btgjd,bkgd->bgjtk/dot_general | solution.py:76
  71.3 1.5 %convolution_bitcast_fusion = f32[4,640,1,128]{3,1,0,2:T(8,128)S(1)} fusion(bf16[4,8,128,640]{2,3,1,0:T(8,128)(2,1)S(1)} %fusion.17, bf16[4,128,8,128]{3,2,1,0:T(8,128)(2,1)S(1)} %bitcast.411), kind=kOutput, calls=%fused_computation.47 | convolution fusion | flops 671088640 | bytes 7602176 | tf_op jit(solution)/shard_map/bgjtk,btgjd->bkgd/dot_general | solution.py:85
  73.0 0.7 slice_bitcast_fusion.7
  73.9 4.6 %collective-permute-start.2 = (bf16[1,2,512,128]{3,2,1,0:T(8,128)(2,1)S(1)}, bf16[1,2,512,128]{3,2,1,0:T(8,128)(2,1)S(1)}, u32[]{:S(2)}, u32[]{:S(2)}) collective-permute-start(bf16[1,2,512,128]{3,2,1,0:T(8,128)(2,1)S(1)} %fusion.76), channel_id=1, source_target_pairs={{0,4},{4,8},{8,12},{12,16},{16,20},{20,24},{24,28},{1,5},{5,9},{9,... | collective-permute-start | bytes 786440 | tf_op jit(solution)/shard_map/ppermute | solution.py:19
  78.5 1.0 slice_bitcast_fusion.12
  79.9 1.6 %fusion.9 = (f32[4,8,128]{2,1,0:T(8,128)S(1)}, f32[4,640,128,8]{2,1,3,0:T(8,128)S(1)}) fusion(pred[4,128,640]{1,2,0:T(8,128)(4,1)S(1)} %get-tuple-element.149, bf16[4,128,8,128]{3,2,1,0:T(8,128)(2,1)S(1)} %bitcast.408, bf16[4,640,1,128]{3,1,0,2:T(8,128)(2,1)S(1)} %constant_dynamic-update-slice_fusion), kind=kOutput, calls=%fused_computation.15 | convolution fusion | flops 678948864 | bytes 12533760 | tf_op jit(solution)/shard_map/btgjd,bkgd->bgjtk/dot_general | solution.py:65
  81.6 2.4 %fusion.13 = f32[4,8,128]{2,1,0:T(8,128)S(1)} fusion(f32[4,640,128,8]{2,1,3,0:T(8,128)S(1)} %get-tuple-element.154, f32[4,8,128]{2,1,0:T(8,128)S(1)} %get-tuple-element.153, pred[4,128,640]{1,2,0:T(8,128)(4,1)S(1)} %get-tuple-element.149), kind=kLoop, calls=%fused_computation.19 | loop fusion | flops 10481664 | bytes 10846208 | tf_op jit(solution)/shard_map/reduce_sum | solution.py:70
  84.0 4.2 %fusion.38 = f32[4,640,1,128]{3,1,0,2:T(8,128)S(1)} fusion(bf16[4,128,8,128]{3,2,1,0:T(8,128)(2,1)} %bitcast.435, f32[4,8,128]{2,1,0:T(8,128)S(1)} %fusion.13, f32[4,8,128]{2,1,0:T(8,128)S(1)} %get-tuple-element.153, f32[4,640,128,8]{2,1,3,0:T(8,128)S(1)} %get-tuple-element.154, pred[4,128,640]{1,2,0:T(8,128)(4,1)S(1)} %get-tuple-element.149), kind=kOutput, calls=%fused_computation.49 | convolution fusion | flops 684195840 | bytes 13205504 | tf_op jit(solution)/shard_map/bgjtk,btgjd->bkgd/dot_general | solution.py:88
  88.3 4.4 %fusion.31 = f32[4,128,8]{1,2,0:T(8,128)S(1)} fusion(f32[4,128,1,8,128]{1,4,3,0,2:T(8,128)S(1)} %copy-done.5, bf16[4,640,1,128]{3,1,0,2:T(8,128)(2,1)} %copy-done.14, f32[4,8,128]{2,1,0:T(8,128)S(1)} %fusion.13, f32[4,8,128]{2,1,0:T(8,128)S(1)} %get-tuple-element.153, f32[4,640,128,8]{2,1,3,0:T(8,128)S(1)} %get-tuple-element.154, ...), kind=kOutput, calls=%fused_computation.40 | convolution fusion | flops 686288896 | bytes 13615104 | tf_op jit(solution)/shard_map/bgjtk,bkgd->btgjd/dot_general | solution.py:72
  92.7 4.2 %fusion.16 = bf16[4,8,128,640]{2,3,1,0:T(8,128)(2,1)S(1)} fusion(f32[4,8,128]{2,1,0:T(8,128)S(1)} %bitcast.467, f32[4,8,128]{2,1,0:T(8,128)S(1)} %fusion.13, f32[4,8,128]{2,1,0:T(8,128)S(1)} %get-tuple-element.153, f32[4,640,128,8]{2,1,3,0:T(8,128)S(1)} %get-tuple-element.154, pred[4,128,640]{1,2,0:T(8,128)(4,1)S(1)} %get-tuple-element.149, ...), kind=kOutput, calls=%fused_computation.22 | convolution fusion | flops 692060160 | bytes 17809408 | tf_op jit(solution)/shard_map/btgjd,bkgd->bgjtk/dot_general | solution.py:76
  97.1 2.1 %copy-done = bf16[4,8,128,640]{2,3,1,0:T(8,128)(2,1)} copy-done((bf16[4,8,128,640]{2,3,1,0:T(8,128)(2,1)}, bf16[4,8,128,640]{2,3,1,0:T(8,128)(2,1)S(1)}, u32[]{:S(2)}) %copy-start) | copy-done | bytes 5242904
  99.2 1.5 %convolution_bitcast_fusion.1 = f32[4,640,1,128]{3,1,0,2:T(8,128)S(1)} fusion(bf16[4,8,128,640]{2,3,1,0:T(8,128)(2,1)S(1)} %fusion.16, bf16[4,128,8,128]{3,2,1,0:T(8,128)(2,1)S(1)} %bitcast.409), kind=kOutput, calls=%fused_computation.48 | convolution fusion | flops 671088640 | bytes 7602176 | tf_op jit(solution)/shard_map/bgjtk,btgjd->bkgd/dot_general | solution.py:85
  101.0 0.8 copy-done.8
  101.8 1.6 %collective-permute-start.3 = (bf16[1,2,512,128]{3,2,1,0:T(8,128)(2,1)S(1)}, bf16[1,2,512,128]{3,2,1,0:T(8,128)(2,1)S(1)}, u32[]{:S(2)}, u32[]{:S(2)}) collective-permute-start(bf16[1,2,512,128]{3,2,1,0:T(8,128)(2,1)S(1)} %maximum_bitcast_fusion.2), channel_id=1, source_target_pairs={{4,0},{8,4},{12,8},{16,12},{20,16},{24,20},{28,24},{5,1},{9,5},{13... | collective-permute-start | bytes 786440 | tf_op jit(solution)/shard_map/ppermute | solution.py:21
  103.3 2.0 %fusion.45 = bf16[4,128,1,8,128]{1,4,3,0,2:T(8,128)(2,1)} fusion(bf16[4,8,128,640]{2,3,1,0:T(8,128)(2,1)S(1)} %fusion.17, bf16[4,640,1,128]{3,1,0,2:T(8,128)(2,1)S(1)} %constant_dynamic-update-slice_fusion.10), kind=kOutput, calls=%fused_computation.52 | convolution fusion | flops 671612928 | bytes 6946816 | tf_op jit(solution)/shard_map/bgjtk,bkgd->btgjd/dot_general | solution.py:82
  105.4 1.7 %copy.66 = bf16[4,128,1,8,128]{4,3,1,0,2:T(8,128)(2,1)S(1)} copy(bf16[4,128,1,8,128]{1,4,3,0,2:T(8,128)(2,1)} %fusion.45) | data formatting | bytes 2097152 | tf_op jit(solution)/shard_map/convert_element_type | solution.py:84
  107.0 1.3 stack_reshape.7
  108.3 2.4 %collective-permute-done.3 = bf16[1,2,512,128]{3,2,1,0:T(8,128)(2,1)S(1)} collective-permute-done((bf16[1,2,512,128]{3,2,1,0:T(8,128)(2,1)S(1)}, bf16[1,2,512,128]{3,2,1,0:T(8,128)(2,1)S(1)}, u32[]{:S(2)}, u32[]{:S(2)}) %collective-permute-start.3) | collective-permute-done | bytes 262176 | tf_op jit(solution)/shard_map/ppermute | solution.py:21
  110.7 1.1 fusion.79
  111.8 1.0 fusion.78
  112.8 1.0 copy.74
  113.8 3.4 %all-to-all-start.3 = ((bf16[1,2,512,128]{3,1,0,2:T(2,128)(2,1)}), bf16[1,2,512,128]{3,1,0,2:T(2,128)(2,1)S(1)}, u32[]{:S(2)}, u32[]{:S(2)}) async-start(bf16[1,2,512,128]{3,1,0,2:T(2,128)(2,1)} %copy.74), calls=%async_computation.3 | async-start | bytes 524288 | tf_op jit(solution)/shard_map/all_to_all | solution.py:165
  117.3 1.2 add_convert_fusion
  118.5 0.2 copy.72
  118.7 1.3 maximum_bitcast_fusion.3
  120.0 3.2 %all-to-all-done.3 = bf16[1,2,512,128]{3,1,0,2:T(2,128)(2,1)S(1)} async-done(((bf16[1,2,512,128]{3,1,0,2:T(2,128)(2,1)}), bf16[1,2,512,128]{3,1,0,2:T(2,128)(2,1)S(1)}, u32[]{:S(2)}, u32[]{:S(2)}) %all-to-all-start.3) | async-done | bytes 262176 | tf_op jit(solution)/shard_map/all_to_all | solution.py:165
  123.2 3.4 %all-to-all-start.2 = ((bf16[1,2,512,128]{3,1,0,2:T(2,128)(2,1)}), bf16[1,2,512,128]{3,1,0,2:T(2,128)(2,1)S(1)}, u32[]{:S(2)}, u32[]{:S(2)}) async-start(bf16[1,2,512,128]{3,1,0,2:T(2,128)(2,1)} %maximum_bitcast_fusion.3), calls=%async_computation.2 | async-start | bytes 524288 | tf_op jit(solution)/shard_map/all_to_all | solution.py:164
  126.7 4.5 %fusion.44 = bf16[4,128,1,8,128]{1,4,3,0,2:T(8,128)(2,1)} fusion(bf16[4,8,128,640]{2,3,1,0:T(8,128)(2,1)} %copy-done, bf16[4,640,1,128]{3,1,0,2:T(8,128)(2,1)S(1)} %constant_dynamic-update-slice_fusion), kind=kOutput, calls=%fused_computation.51 | convolution fusion | flops 671612928 | bytes 6946816 | tf_op jit(solution)/shard_map/bgjtk,bkgd->btgjd/dot_general | solution.py:82
  131.2 1.7 %copy.58 = bf16[4,128,1,8,128]{4,3,1,0,2:T(8,128)(2,1)S(1)} copy(bf16[4,128,1,8,128]{1,4,3,0,2:T(8,128)(2,1)} %fusion.44) | data formatting | bytes 2097152 | tf_op jit(solution)/shard_map/convert_element_type | solution.py:84
  132.9 1.3 stack_reshape.6
  134.1 2.7 %maximum_bitcast_fusion = bf16[1,2,512,1024]{3,2,1,0:T(8,128)(2,1)} fusion(bf16[1,512,1024]{2,1,0:T(8,128)(2,1)S(1)} %copy-done.1, bf16[1,512,1024]{2,1,0:T(8,128)(2,1)} %stack_reshape.6), kind=kLoop, calls=%fused_computation.34 | loop fusion | flops 1048576 | bytes 4194304 | tf_op jit(solution)/shard_map/broadcast_in_dim | solution.py:160
  136.9 0.2 copy.75
  137.1 0.8 all_to_all.67
  137.9 0.2 copy.73
  138.1 0.8 all_to_all.63
  (84 shorter events, 2.3 us)
Async XLA Ops:
  2.5 13.4 %all-to-all-start = ((bf16[1,2,128,512]{2,1,0,3:T(2,128)(2,1)}), bf16[1,2,128,512]{2,1,0,3:T(2,128)(2,1)S(1)}, u32[]{:S(2)}, u32[]{:S(2)}) async-start(bf16[1,2,128,512]{2,1,0,3:T(2,128)(2,1)} %copy.46), calls=%async_computation | async-start | bytes 524288 | tf_op jit(solution)/shard_map/all_to_all | solution.py:100
  15.9 9.5 %all-to-all-start.1 = ((bf16[1,2,128,512]{2,1,0,3:T(2,128)(2,1)}), bf16[1,2,128,512]{2,1,0,3:T(2,128)(2,1)S(1)}, u32[]{:S(2)}, u32[]{:S(2)}) async-start(bf16[1,2,128,512]{2,1,0,3:T(2,128)(2,1)} %copy.48), calls=%async_computation.1 | async-start | bytes 524288 | tf_op jit(solution)/shard_map/all_to_all | solution.py:101
  27.3 20.7 %collective-permute-start.1 = (bf16[1,2,512,128]{3,2,1,0:T(8,128)(2,1)}, bf16[1,2,512,128]{3,2,1,0:T(8,128)(2,1)}, u32[]{:S(2)}, u32[]{:S(2)}) collective-permute-start(bf16[1,2,512,128]{3,2,1,0:T(8,128)(2,1)} %maximum_bitcast_fusion.1), channel_id=1, source_target_pairs={{4,0},{8,4},{12,8},{16,12},{20,16},{24,20},{28,24},{5,1},{9,5},{13... | collective-permute-start | bytes 786440 | tf_op jit(solution)/shard_map/ppermute | solution.py:21
  49.8 28.6 %collective-permute-start = (bf16[1,2,512,128]{3,2,1,0:T(8,128)(2,1)}, bf16[1,2,512,128]{3,2,1,0:T(8,128)(2,1)}, u32[]{:S(2)}, u32[]{:S(2)}) collective-permute-start(bf16[1,2,512,128]{3,2,1,0:T(8,128)(2,1)} %get-tuple-element.137), channel_id=1, source_target_pairs={{0,4},{4,8},{8,12},{12,16},{16,20},{20,24},{24,28},{1,5},{5,9},{9,... | collective-permute-start | bytes 786440 | tf_op jit(solution)/shard_map/ppermute | solution.py:19
  60.6 3.1 %copy-start.6 = (f32[4,128,1,8,128]{1,4,3,0,2:T(8,128)S(1)}, f32[4,128,1,8,128]{1,4,3,0,2:T(8,128)}, u32[]{:S(2)}) copy-start(f32[4,128,1,8,128]{1,4,3,0,2:T(8,128)} %copy.63) | copy-start | bytes 6291460
  71.1 8.4 %copy-start.11 = (bf16[512,128]{1,0:T(8,128)(2,1)S(1)}, bf16[512,128]{1,0:T(8,128)(2,1)}, u32[]{:S(2)}) copy-start(bf16[512,128]{1,0:T(8,128)(2,1)} %get-tuple-element.117) | copy-start | bytes 393220
  71.1 8.5 %copy-start.10 = (bf16[512,128]{1,0:T(8,128)(2,1)S(1)}, bf16[512,128]{1,0:T(8,128)(2,1)}, u32[]{:S(2)}) copy-start(bf16[512,128]{1,0:T(8,128)(2,1)} %get-tuple-element.158) | copy-start | bytes 393220
  71.3 8.5 %copy-start.13 = (bf16[1,1,512,128]{3,2,1,0:T(8,128)(2,1)S(1)}, bf16[1,1,512,128]{3,2,1,0:T(8,128)(2,1)}, u32[]{:S(2)}) copy-start(bf16[1,1,512,128]{3,2,1,0:T(8,128)(2,1)} %get-tuple-element.160) | copy-start | bytes 393220
  71.3 8.6 %copy-start.12 = (bf16[1,1,512,128]{3,2,1,0:T(8,128)(2,1)S(1)}, bf16[1,1,512,128]{3,2,1,0:T(8,128)(2,1)}, u32[]{:S(2)}) copy-start(bf16[1,1,512,128]{3,2,1,0:T(8,128)(2,1)} %get-tuple-element.115) | copy-start | bytes 393220
  73.8 7.8 %copy-start.2 = (f32[1,512,128]{2,1,0:T(8,128)}, f32[1,512,128]{2,1,0:T(8,128)S(1)}, u32[]{:S(2)}) copy-start(f32[1,512,128]{2,1,0:T(8,128)S(1)} %get-tuple-element.113) | copy-start | bytes 786436
  73.8 7.8 %copy-start.4 = (f32[1024,1,128]{2,0,1:T(8,128)}, f32[1024,1,128]{2,0,1:T(8,128)S(1)}, u32[]{:S(2)}) copy-start(f32[1024,1,128]{2,0,1:T(8,128)S(1)} %pad_add_fusion.1) | copy-start | bytes 1572868
  73.9 34.4 %collective-permute-start.2 = (bf16[1,2,512,128]{3,2,1,0:T(8,128)(2,1)S(1)}, bf16[1,2,512,128]{3,2,1,0:T(8,128)(2,1)S(1)}, u32[]{:S(2)}, u32[]{:S(2)}) collective-permute-start(bf16[1,2,512,128]{3,2,1,0:T(8,128)(2,1)S(1)} %fusion.76), channel_id=1, source_target_pairs={{0,4},{4,8},{8,12},{12,16},{16,20},{20,24},{24,28},{1,5},{5,9},{9,... | collective-permute-start | bytes 786440 | tf_op jit(solution)/shard_map/ppermute | solution.py:19
  79.8 4.2 %copy-start.14 = (bf16[4,640,1,128]{3,1,0,2:T(8,128)(2,1)}, bf16[4,640,1,128]{3,1,0,2:T(8,128)(2,1)S(1)}, u32[]{:S(2)}) copy-start(bf16[4,640,1,128]{3,1,0,2:T(8,128)(2,1)S(1)} %constant_dynamic-update-slice_fusion.5) | copy-start | bytes 1966084
  84.0 4.2 %copy-start.5 = (f32[4,128,1,8,128]{1,4,3,0,2:T(8,128)S(1)}, f32[4,128,1,8,128]{1,4,3,0,2:T(8,128)}, u32[]{:S(2)}) copy-start(f32[4,128,1,8,128]{1,4,3,0,2:T(8,128)} %copy.55) | copy-start | bytes 6291460
  88.2 4.4 %copy-start.9 = (bf16[64,8,8,128]{3,2,1,0:T(8,128)(2,1)S(1)}, bf16[64,8,8,128]{3,2,1,0:T(8,128)(2,1)}, u32[]{:S(2)}) copy-start(bf16[64,8,8,128]{3,2,1,0:T(8,128)(2,1)} %copy.101) | copy-start | bytes 3145732
  88.3 4.4 %copy-start.15 = (bf16[4,640,1,128]{3,1,0,2:T(8,128)(2,1)S(1)}, bf16[4,640,1,128]{3,1,0,2:T(8,128)(2,1)}, u32[]{:S(2)}) copy-start(bf16[4,640,1,128]{3,1,0,2:T(8,128)(2,1)} %copy-done.14) | copy-start | bytes 1966084
  96.9 2.3 %copy-start = (bf16[4,8,128,640]{2,3,1,0:T(8,128)(2,1)}, bf16[4,8,128,640]{2,3,1,0:T(8,128)(2,1)S(1)}, u32[]{:S(2)}) copy-start(bf16[4,8,128,640]{2,3,1,0:T(8,128)(2,1)S(1)} %fusion.16) | copy-start | bytes 15728644
  97.1 6.2 %copy-start.7 = (f32[1024,1,128]{2,0,1:T(8,128)}, f32[1024,1,128]{2,0,1:T(8,128)S(1)}, u32[]{:S(2)}) copy-start(f32[1024,1,128]{2,0,1:T(8,128)S(1)} %pad_add_fusion) | copy-start | bytes 1572868
  100.7 9.9 %copy-start.3 = (f32[1,512,128]{2,1,0:T(8,128)S(1)}, f32[1,512,128]{2,1,0:T(8,128)}, u32[]{:S(2)}) copy-start(f32[1,512,128]{2,1,0:T(8,128)} %copy-done.2) | copy-start | bytes 786436
  100.9 0.8 copy-start.8
  101.8 8.9 %collective-permute-start.3 = (bf16[1,2,512,128]{3,2,1,0:T(8,128)(2,1)S(1)}, bf16[1,2,512,128]{3,2,1,0:T(8,128)(2,1)S(1)}, u32[]{:S(2)}, u32[]{:S(2)}) collective-permute-start(bf16[1,2,512,128]{3,2,1,0:T(8,128)(2,1)S(1)} %maximum_bitcast_fusion.2), channel_id=1, source_target_pairs={{4,0},{8,4},{12,8},{16,12},{20,16},{24,20},{28,24},{5,1},{9,5},{13... | collective-permute-start | bytes 786440 | tf_op jit(solution)/shard_map/ppermute | solution.py:21
  108.3 25.8 %copy-start.1 = (bf16[1,512,1024]{2,1,0:T(8,128)(2,1)S(1)}, bf16[1,512,1024]{2,1,0:T(8,128)(2,1)}, u32[]{:S(2)}) copy-start(bf16[1,512,1024]{2,1,0:T(8,128)(2,1)} %stack_reshape.7) | copy-start | bytes 3145732
  113.8 9.4 %all-to-all-start.3 = ((bf16[1,2,512,128]{3,1,0,2:T(2,128)(2,1)}), bf16[1,2,512,128]{3,1,0,2:T(2,128)(2,1)S(1)}, u32[]{:S(2)}, u32[]{:S(2)}) async-start(bf16[1,2,512,128]{3,1,0,2:T(2,128)(2,1)} %copy.74), calls=%async_computation.3 | async-start | bytes 524288 | tf_op jit(solution)/shard_map/all_to_all | solution.py:165
  123.2 14.7 %all-to-all-start.2 = ((bf16[1,2,512,128]{3,1,0,2:T(2,128)(2,1)}), bf16[1,2,512,128]{3,1,0,2:T(2,128)(2,1)S(1)}, u32[]{:S(2)}, u32[]{:S(2)}) async-start(bf16[1,2,512,128]{3,1,0,2:T(2,128)(2,1)} %maximum_bitcast_fusion.3), calls=%async_computation.2 | async-start | bytes 524288 | tf_op jit(solution)/shard_map/all_to_all | solution.py:164
where the time goes:
time: 140 us; the launch traced here: 139 us
  local copies, waits for them, and re-layouts  39.6 us (28%)
  matrix products  36.2 us (26%)
  starting transfers between devices  27.2 us (19%)
  other arithmetic  23.7 us (17%)
  waiting for transfers between devices  10.7 us (8%)
    unnamed x57, local copies, waits for them, and re-layouts  19.9 us
    ppermute x2, starting transfers between devices, padded_2(): lax.ppermute(tail, axis, [(i, (i + 1) % count) for i in range(ends)])  9.92 us
    dot_general x2, matrix products, span_grads(): jnp.einsum('btgjd,bkgd->bgjtk', do_blocks, v_windows, preferred_element_t...  8.42 us
    dot_general x2, matrix products, span_grads(): jnp.einsum('bgjtk,bkgd->btgjd', probs_b, v_windows, preferred_element_typ...  7.54 us
    dot_general x2, matrix products, span_grads(): jnp.einsum('bgjtk,btgjd->bkgd', probs_b, do_blocks, preferred_element_typ...  7.32 us
    dot_general x2, matrix products, span_grads(): jnp.einsum('bgjtk,bkgd->btgjd', dscores, k_windows, preferred_element_typ...  6.55 us
    convert_element_type x2, local copies, waits for them, and re-layouts, span_grads(): do_blocks.astype(jnp.float32) * outputs.astype(jnp.float32)  5.78 us
    all_to_all x1, waiting for transfers between devices, per_device(): lax.all_to_all(value, 'head', split_axis=3, concat_axis=2, tiled=True)  5.15 us
  transfers between devices with their start and end apart: 8, of which 3 were waited for; matrix products, arithmetic and copies ran while one was open for 62% of the time, Pallas kernels for 0%

commit v1 on v0

v1 whole, which is shorter than its diff:
```python
import functools

import jax
import jax.numpy as jnp
from jax import lax
from jax.experimental import pallas as pl
from jax.experimental.pallas import tpu as pltpu
from jax.sharding import PartitionSpec as P

HD = 128
BLK = 128
REACH = 2
SCALE = HD**-0.5
SCALE_LOG2E = SCALE * 1.4426950408889634
BF16 = jnp.bfloat16
F32 = jnp.float32
VMEM = pl.BlockSpec(memory_space=pltpu.VMEM)
SMEM = pl.BlockSpec(memory_space=pltpu.SMEM)


def shape(dims, dtype=BF16):
    return jax.ShapeDtypeStruct(dims, dtype)


def call(body, inputs, outs, scratch=(), flops=0, limit=12, out_spec=VMEM):
    in_specs = [SMEM if a.dtype == jnp.int32 else VMEM for a in inputs]
    size = sum(o.size * o.dtype.itemsize for o in outs)
    return pl.pallas_call(
        body,
        out_shape=outs,
        in_specs=in_specs,
        out_specs=[out_spec] * len(outs),
        scratch_shapes=list(scratch),
        compiler_params=pltpu.CompilerParams(vmem_limit_bytes=limit << 20),
        cost_estimate=pl.CostEstimate(flops=flops, bytes_accessed=size, transcendentals=0),
        name=body.func.__name__,
    )(*inputs)


def lanes(index):
    return pl.ds(pl.multiple_of(index * HD, HD), HD)


def rows(index, blocks=1):
    return pl.ds(pl.multiple_of(index * BLK, BLK), blocks * BLK)


def pack_keys(heads, place, key, value, *sends):
    me, first = place[0], place[1]
    for half in range(2):
        slot = first if half == 0 else 1 - first
        for t in range(1, heads):
            out = sends[half * (heads - 1) + t - 1]
            out[0] = key[0, slot, :, lanes(me ^ t)]
            out[1] = value[0, slot, :, lanes(me ^ t)]


def join_keys(heads, half, place, key, value, *refs):
    received, (span, rim) = refs[: heads - 1], refs[heads - 1 :]
    me = place[0]
    slot = place[1] if half == 0 else 1 - place[1]
    span[0, rows(me), :] = key[0, slot, :, lanes(me)]
    span[1, rows(me), :] = value[0, slot, :, lanes(me)]
    for t in range(1, heads):
        span[0, rows(me ^ t), :] = received[t - 1][0]
        span[1, rows(me ^ t), :] = received[t - 1][1]
    rim[...] = span[:, (heads - REACH) * BLK :, :]


def dot(a, b, ca, cb):
    return lax.dot_general(a, b, (((ca,), (cb,)), ((), ())), preferred_element_type=F32)


def block_grads(n, first, queries, grads, keys, d_queries, d_keys):
    count = queries.shape[1] // HD
    window = pl.ds(first * BLK, n * BLK)
    k, v = keys[0, window, :], keys[1, window, :]
    q = jnp.concatenate([queries[:, j * HD : (j + 1) * HD] for j in range(count)], axis=0)
    do = jnp.concatenate([grads[:, j * HD : (j + 1) * HD] for j in range(count)], axis=0)
    s = dot(k, q, 1, 1)
    dp = dot(v, do, 1, 1)
    token = lax.broadcasted_iota(jnp.int32, (BLK, count * BLK), 1) & (BLK - 1)
    seen = lax.broadcasted_iota(jnp.int32, (BLK, count * BLK), 0) <= token
    last = jnp.where(seen, s[(n - 1) * BLK :], -jnp.inf)
    s = jnp.concatenate([s[: (n - 1) * BLK], last], axis=0) if n > 1 else last
    peak = jnp.max(s, axis=0, keepdims=True)
    w = jnp.exp2((s - peak) * SCALE_LOG2E)
    inverse = 1.0 / jnp.sum(w, axis=0, keepdims=True)
    delta = jnp.sum(w * dp, axis=0, keepdims=True) * inverse
    p = w * inverse
    ds = (p * (dp - delta)).astype(BF16)
    d_keys[0, window, :] += dot(ds, q, 1, 0) * SCALE
    d_keys[1, window, :] += dot(p.astype(BF16), do, 1, 0)
    dq = (dot(k.T, ds, 1, 0) * SCALE).astype(BF16)
    for j in range(count):
        d_queries[:, j * HD : (j + 1) * HD] = dq[:, j * BLK : (j + 1) * BLK].T


def span_part(first_block, blocks, per_span, half, place, doc_start, query, d_out, keys, d_query, d_keys):
    slot = place[1] if half == 0 else 1 - place[1]
    span = place[3] if half == 0 else place[4]
    d_keys[...] = jnp.zeros_like(d_keys)
    for b in range(blocks):
        block = span * per_span + first_block + b
        here = doc_start[block]
        before = doc_start[jnp.maximum(block - 1, 0)]
        visible = jnp.where(here == 1, 1, jnp.where(before == 1, 2, 3))
        tokens = pl.ds((first_block + b) * BLK, BLK)
        for n in range(1, REACH + 2):

            @pl.when(visible == n)
            def _(n=n, tokens=tokens, b=b):
                block_grads(
                    n,
                    b + REACH + 1 - n,
                    query.at[0, slot, tokens, :],
                    d_out.at[0, slot, tokens, :],
                    keys,
                    d_query.at[pl.ds(b * BLK, BLK), :],
                    d_keys,
                )


def late_blocks(per_span, half, place, doc_start, query, d_out, keys, d_query, d_keys):
    span_part(REACH, per_span - REACH, per_span, half, place, doc_start, query, d_out, keys, d_query, d_keys)


def early_blocks(per_span, half, place, doc_start, query, d_out, keys, other, incoming, d_query, d_own, d_rim, window, d_window):
    cut = REACH * BLK
    window[:, cut:, :] = keys[:, :cut, :]
    window[:, :cut, :] = incoming[...]
    if half == 1:

        @pl.when(place[2] == 1)
        def _():
            window[:, :cut, :] = other[:, (per_span - REACH) * BLK :, :]

    span_part(0, REACH, per_span, half, place, doc_start, query, d_out, window, d_query, d_window)
    d_rim[...] = d_window[:, :cut, :].astype(BF16)
    d_own[...] = d_window[:, cut:, :]


def store_queries(reach, place, early_first, late_first, early_second, late_second, d_query, sems):
    copies = []
    for half, parts in ((0, (early_first, late_first)), (1, (early_second, late_second))):
        slot = place[1] if half == 0 else 1 - place[1]
        for part, start in zip(parts, (0, reach * BLK)):
            there = d_query.at[0, slot, pl.ds(start, part.shape[0]), :]
            copies.append(pltpu.make_async_copy(part, there, sems.at[len(copies)]))
    for copy in copies:
        copy.start()
    for copy in copies:
        copy.wait()


def pack_grads(heads, half, place, d_late, d_own, d_back, d_local, *refs):
    sends, total = refs[:-1], refs[-1]
    me = place[0]
    cut = REACH * BLK
    total[...] = d_late[...]
    total[:, :cut, :] += d_own[...]
    total[:, (heads - REACH) * BLK :, :] += d_back[...].astype(F32)
    if half == 0:

        @pl.when(place[2] == 1)
        def _():
            total[:, (heads - REACH) * BLK :, :] += d_local[...].astype(F32)

    for t in range(heads):
        sends[t][...] = total[:, rows(me ^ t), :].astype(BF16)


def join_grads(heads, place, *refs):
    parts, (d_key, d_value) = refs[: 2 * heads], refs[2 * heads :]
    me = place[0]
    for half in range(2):
        slot = place[1] if half == 0 else 1 - place[1]
        for t in range(heads):
            d_key[0, slot, :, lanes(me ^ t)] = parts[half * heads + t][0]
            d_value[0, slot, :, lanes(me ^ t)] = parts[half * heads + t][1]


def per_device(query, key, value, d_out, doc_start):
    ctx, ctx_count = lax.axis_index("ctx"), lax.axis_size("ctx")
    head, heads = lax.axis_index("head"), lax.axis_size("head")
    odd = ctx % 2
    first = 1 - odd
    is_last = (ctx == ctx_count - 1).astype(jnp.int32)
    spans = [ctx, 2 * ctx_count - 1 - ctx]
    span_first = jnp.where(first == 0, spans[0], spans[1])
    span_second = spans[0] + spans[1] - span_first
    place = jnp.stack([head, first, is_last, span_first, span_second]).astype(jnp.int32)
    block = shape((2, BLK, HD))
    partners = range(1, heads)
    swap = lambda x, t: lax.ppermute(x, "head", [(i, i ^ t) for i in range(heads)])
    outer = [p for i in range(1, ctx_count - 1, 2) for p in ((i, i + 1), (i + 1, i))]
    inner = [p for i in range(0, ctx_count, 2) for p in ((i, i + 1), (i + 1, i))]
    to_outer = lambda x: lax.ppermute(x, "ctx", outer)
    to_inner = lambda x: lax.ppermute(x, "ctx", inner)

    sends = call(functools.partial(pack_keys, heads), (place, key, value), [block] * (2 * (heads - 1)))
    received = [
        [swap(sends[half * (heads - 1) + t - 1], t) for t in partners] for half in range(2)
    ]
    joined = [
        call(
            functools.partial(join_keys, heads, half),
            (place, key, value, *received[half]),
            [shape((2, heads * BLK, HD)), shape((2, REACH * BLK, HD))],
        )
        for half in range(2)
    ]
    keys = [j[0] for j in joined]
    rim_second = to_outer(joined[0][1])
    rim_first = to_inner(joined[1][1])
    flops = 8 * BLK * BLK * HD * (query.shape[3] // HD) * REACH * (REACH + 1)

    def late(half):
        return call(
            functools.partial(late_blocks, heads, half),
            (place, doc_start, query, d_out, keys[half]),
            [shape(((heads - REACH) * BLK, query.shape[3])), shape((2, heads * BLK, HD), F32)],
            flops=flops,
            limit=20,
        )

    def early(half, incoming):
        return call(
            functools.partial(early_blocks, heads, half),
            (place, doc_start, query, d_out, keys[half], keys[1 - half], incoming),
            [
                shape((REACH * BLK, query.shape[3])),
                shape((2, REACH * BLK, HD), F32),
                shape((2, REACH * BLK, HD)),
            ],
            scratch=[
                pltpu.VMEM((2, 2 * REACH * BLK, HD), BF16),
                pltpu.VMEM((2, 2 * REACH * BLK, HD), F32),
            ],
            flops=flops,
            limit=20,
        )

    dq_late_first, late_first = late(0)
    dq_early_second, own_second, edge_second = early(1, rim_second)
    back_first = to_outer(edge_second)
    dq_early_first, own_first, edge_first = early(0, rim_first)
    back_second = to_inner(edge_first)
    dq_late_second, late_second = late(1)
    d_query = call(
        functools.partial(store_queries, REACH),
        (place, dq_early_first, dq_late_first, dq_early_second, dq_late_second),
        [shape(query.shape)],
        scratch=[pltpu.SemaphoreType.DMA((4,))],
        out_spec=pl.BlockSpec(memory_space=pl.ANY),
    )[0]

    def finish(half, d_late, d_own, d_back, d_local):
        parts = call(
            functools.partial(pack_grads, heads, half),
            (place, d_late, d_own, d_back, d_local),
            [block] * heads,
            scratch=[pltpu.VMEM((2, heads * BLK, HD), F32)],
        )
        return [parts[0]] + [swap(parts[t], t) for t in partners]

    parts_first = finish(0, late_first, own_first, back_first, edge_second)
    parts_second = finish(1, late_second, own_second, back_second, edge_first)
    d_key, d_value = call(
        functools.partial(join_grads, heads),
        (place, *parts_first, *parts_second),
        [shape(key.shape), shape(value.shape)],
    )
    return d_query, d_key, d_value


def solution(mesh):
    tokens = P("ctx", None, "head", None)
    columns = P("ctx", None, None, "head")
    return jax.shard_map(
        per_device,
        mesh=mesh,
        in_specs=(columns, tokens, tokens, columns, P()),
        out_specs=(columns, tokens, tokens),
        check_vma=False,
    )
```

time: 140 us -> 52.7 us (0.38)
  the two profiles are of different devices: /device:TPU:0 before, /device:TPU:13 now
where the time goes in v1:
time: 52.7 us; the launch traced here: 52.4 us
  Pallas kernels  18.5 us (35%)
  starting transfers between devices  18.1 us (34%)
  waiting for transfers between devices  9.13 us (17%)
  local copies, waits for them, and re-layouts  5.83 us (11%)
  between operations  0.85 us (2%)
    pallas_call x11, Pallas kernels, call(): pl.pallas_call(body, out_shape=outs, in_specs=in_specs, out_specs=[out_sp...  18.5 us
    ppermute x12, starting transfers between devices, per_device(): lax.ppermute(x, 'head', [(i, i ^ t) for i in range(heads)])  9.61 us
    ppermute x12, waiting for transfers between devices, per_device(): lax.ppermute(x, 'head', [(i, i ^ t) for i in range(heads)])  9.12 us
    ppermute x2, starting transfers between devices, per_device(): to_outer = lambda x: lax.ppermute(x, 'ctx', outer)  8.13 us
    unnamed x14, local copies, waits for them, and re-layouts  5.74 us
  transfers between devices with their start and end apart: 16, of which 6 were waited for; matrix products, arithmetic and copies ran while one was open for 0% of the time, Pallas kernels for 30%

profile of v1, /device:TPU:13, one launch (start us, length us, event | category | flops | bytes accessed | tf_op | source)
XLA Modules:
  0.0 52.4 jit_solution(17931100944139082567)
XLA Ops:
  0.6 0.1 stack.27.place
  0.7 0.0 copy-start.4
  0.7 0.9 %copy-done.4 = bf16[1,2,128,512]{3,2,1,0:T(8,128)(2,1)S(1)} copy-done((bf16[1,2,128,512]{3,2,1,0:T(8,128)(2,1)S(1)}, bf16[1,2,128,512]{3,2,1,0:T(8,128)(2,1)}, u32[]{:S(2)}) %copy-start.4) | copy-done | bytes 262168
  1.7 0.0 copy-start.5
  1.7 0.9 %copy-done.5 = bf16[1,2,128,512]{3,2,1,0:T(8,128)(2,1)S(1)} copy-done((bf16[1,2,128,512]{3,2,1,0:T(8,128)(2,1)S(1)}, bf16[1,2,128,512]{3,2,1,0:T(8,128)(2,1)}, u32[]{:S(2)}) %copy-start.5) | copy-done | bytes 262168
  2.6 0.6 %pack_keys.1 = (bf16[2,128,128]{2,1,0:T(8,128)(2,1)S(1)}, bf16[2,128,128]{2,1,0:T(8,128)(2,1)S(1)}, bf16[2,128,128]{2,1,0:T(8,128)(2,1)S(1)}, bf16[2,128,128]{2,...) custom-call(s32[5]{0:T(128)S(1)} %stack.27.place, ...), custom_call_target="tpu_custom_call" | custom-call | bytes 393216 | tf_op jit(solution)/shard_map/pack_keys/pallas_call | solution.py:28
  3.3 0.7 %collective-permute-start.3 = (bf16[2,128,128]{2,1,0:T(8,128)(2,1)S(1)}, bf16[2,128,128]{2,1,0:T(8,128)(2,1)S(1)}, u32[]{:S(2)}, u32[]{:S(2)}) collective-permute-start(bf16[2,128,128]{2,1,0:T(8,128)(2,1)S(1)} %get-tuple-element.37), channel_id=1, source_target_pairs={{0,1},{1,0},{2,3},{3,2},{4,5},{5,4},{6,7},{7,6},{8,9},{9,8},{10,11... | collective-permute-start | bytes 196616 | tf_op jit(solution)/shard_map/ppermute | solution.py:195
  4.0 1.2 %collective-permute-start.4 = (bf16[2,128,128]{2,1,0:T(8,128)(2,1)S(1)}, bf16[2,128,128]{2,1,0:T(8,128)(2,1)S(1)}, u32[]{:S(2)}, u32[]{:S(2)}) collective-permute-start(bf16[2,128,128]{2,1,0:T(8,128)(2,1)S(1)} %get-tuple-element.38), channel_id=1, source_target_pairs={{0,2},{1,3},{2,0},{3,1},{4,6},{5,7},{6,4},{7,5},{8,10},{9,11},{10,... | collective-permute-start | bytes 196616 | tf_op jit(solution)/shard_map/ppermute | solution.py:195
  5.2 0.5 collective-permute-start.5
  5.7 0.0 collective-permute-done.3.refs_0_
  5.7 2.0 %collective-permute-done.4.refs_1_ = bf16[2,128,128]{2,1,0:T(8,128)(2,1)S(1)} collective-permute-done((bf16[2,128,128]{2,1,0:T(8,128)(2,1)S(1)}, bf16[2,128,128]{2,1,0:T(8,128)(2,1)S(1)}, u32[]{:S(2)}, u32[]{:S(2)}) %collective-permute-start.4) | collective-permute-done | bytes 65568 | tf_op jit(solution)/shard_map/ppermute | solution.py:195
  7.7 1.6 %collective-permute-done.5.refs_2_ = bf16[2,128,128]{2,1,0:T(8,128)(2,1)S(1)} collective-permute-done((bf16[2,128,128]{2,1,0:T(8,128)(2,1)S(1)}, bf16[2,128,128]{2,1,0:T(8,128)(2,1)S(1)}, u32[]{:S(2)}, u32[]{:S(2)}) %collective-permute-start.5) | collective-permute-done | bytes 65568 | tf_op jit(solution)/shard_map/ppermute | solution.py:195
  9.3 0.6 %join_keys.3 = (bf16[2,512,128]{2,1,0:T(8,128)(2,1)S(1)}, bf16[2,256,128]{2,1,0:T(8,128)(2,1)S(1)}) custom-call(s32[5]{0:T(128)S(1)} %stack.27.place, bf16[1,2,128,512]{3,2,1,0:T(8,128)(2,1)S(1)} %copy-done.4, bf16[1,2,128,512]{3,2,1,0:T(8,128)(2,1)S(1)} %copy-done.5, bf16[2,128,128]{2,1,0:T(8,128)(2,1)S(1)} %collective-permute-done.3.refs_0_, ...), custom_call_target="tpu_custom_call" | custom-call | bytes 393216 | tf_op jit(solution)/shard_map/join_keys/pallas_call | solution.py:28
  9.9 0.3 collective-permute-start.6
  10.2 0.6 %collective-permute-start = (bf16[2,128,128]{2,1,0:T(8,128)(2,1)S(1)}, bf16[2,128,128]{2,1,0:T(8,128)(2,1)S(1)}, u32[]{:S(2)}, u32[]{:S(2)}) collective-permute-start(bf16[2,128,128]{2,1,0:T(8,128)(2,1)S(1)} %get-tuple-element.33), channel_id=1, source_target_pairs={{0,1},{1,0},{2,3},{3,2},{4,5},{5,4},{6,7},{7,6},{8,9},{9,8},{10,11... | collective-permute-start | bytes 196616 | tf_op jit(solution)/shard_map/ppermute | solution.py:195
  10.8 1.1 %collective-permute-start.1 = (bf16[2,128,128]{2,1,0:T(8,128)(2,1)S(1)}, bf16[2,128,128]{2,1,0:T(8,128)(2,1)S(1)}, u32[]{:S(2)}, u32[]{:S(2)}) collective-permute-start(bf16[2,128,128]{2,1,0:T(8,128)(2,1)S(1)} %get-tuple-element.34), channel_id=1, source_target_pairs={{0,2},{1,3},{2,0},{3,1},{4,6},{5,7},{6,4},{7,5},{8,10},{9,11},{10,... | collective-permute-start | bytes 196616 | tf_op jit(solution)/shard_map/ppermute | solution.py:195
  11.8 0.6 %collective-permute-start.2 = (bf16[2,128,128]{2,1,0:T(8,128)(2,1)S(1)}, bf16[2,128,128]{2,1,0:T(8,128)(2,1)S(1)}, u32[]{:S(2)}, u32[]{:S(2)}) collective-permute-start(bf16[2,128,128]{2,1,0:T(8,128)(2,1)S(1)} %get-tuple-element.35), channel_id=1, source_target_pairs={{0,3},{1,2},{2,1},{3,0},{4,7},{5,6},{6,5},{7,4},{8,11},{9,10},{10,... | collective-permute-start | bytes 196616 | tf_op jit(solution)/shard_map/ppermute | solution.py:195
  12.4 0.0 collective-permute-done.refs_0_
  12.4 2.1 %collective-permute-done.1.refs_1_ = bf16[2,128,128]{2,1,0:T(8,128)(2,1)S(1)} collective-permute-done((bf16[2,128,128]{2,1,0:T(8,128)(2,1)S(1)}, bf16[2,128,128]{2,1,0:T(8,128)(2,1)S(1)}, u32[]{:S(2)}, u32[]{:S(2)}) %collective-permute-start.1) | collective-permute-done | bytes 65568 | tf_op jit(solution)/shard_map/ppermute | solution.py:195
  14.5 1.6 %collective-permute-done.2.refs_2_ = bf16[2,128,128]{2,1,0:T(8,128)(2,1)S(1)} collective-permute-done((bf16[2,128,128]{2,1,0:T(8,128)(2,1)S(1)}, bf16[2,128,128]{2,1,0:T(8,128)(2,1)S(1)}, u32[]{:S(2)}, u32[]{:S(2)}) %collective-permute-start.2) | collective-permute-done | bytes 65568 | tf_op jit(solution)/shard_map/ppermute | solution.py:195
  16.1 0.6 %join_keys.2 = (bf16[2,512,128]{2,1,0:T(8,128)(2,1)S(1)}, bf16[2,256,128]{2,1,0:T(8,128)(2,1)S(1)}) custom-call(s32[5]{0:T(128)S(1)} %stack.27.place, bf16[1,2,128,512]{3,2,1,0:T(8,128)(2,1)S(1)} %copy-done.4, bf16[1,2,128,512]{3,2,1,0:T(8,128)(2,1)S(1)} %copy-done.5, bf16[2,128,128]{2,1,0:T(8,128)(2,1)S(1)} %collective-permute-done.refs_0_, ...), custom_call_target="tpu_custom_call" | custom-call | bytes 393216 | tf_op jit(solution)/shard_map/join_keys/pallas_call | solution.py:28
  16.6 4.2 %collective-permute-start.7 = (bf16[2,256,128]{2,1,0:T(8,128)(2,1)S(1)}, bf16[2,256,128]{2,1,0:T(8,128)(2,1)S(1)}, u32[]{:S(2)}, u32[]{:S(2)}) collective-permute-start(bf16[2,256,128]{2,1,0:T(8,128)(2,1)S(1)} %get-tuple-element.44), channel_id=1, source_target_pairs={{4,8},{8,4},{12,16},{16,12},{20,24},{24,20},{5,9},{9,5},{13,17},{1... | collective-permute-start | bytes 393224 | tf_op jit(solution)/shard_map/ppermute | solution.py:198
  20.8 0.0 collective-permute-done.6.incoming
  20.8 0.0 copy-start
  20.8 1.6 %copy-done = bf16[1,2,512,1024]{3,2,1,0:T(8,128)(2,1)S(1)} copy-done((bf16[1,2,512,1024]{3,2,1,0:T(8,128)(2,1)S(1)}, bf16[1,2,512,1024]{3,2,1,0:T(8,128)(2,1)}, u32[]{:S(2)}) %copy-start) | copy-done | bytes 2097176
  22.4 0.0 copy-start.2
  22.4 1.6 %copy-done.2 = bf16[1,2,512,1024]{3,2,1,0:T(8,128)(2,1)S(1)} copy-done((bf16[1,2,512,1024]{3,2,1,0:T(8,128)(2,1)S(1)}, bf16[1,2,512,1024]{3,2,1,0:T(8,128)(2,1)}, u32[]{:S(2)}) %copy-start.2) | copy-done | bytes 2097176
  24.0 0.0 copy-start.6
  24.0 0.7 %copy-done.6 = s32[64]{0:T(128)S(1)} copy-done((s32[64]{0:T(128)S(1)}, s32[64]{0:T(128)}, u32[]{:S(2)}) %copy-start.6) | copy-done | bytes 280
  24.7 3.5 %early_blocks.2 = (bf16[256,1024]{1,0:T(8,128)(2,1)S(1)}, f32[2,256,128]{2,1,0:T(8,128)S(1)}, bf16[2,256,128]{2,1,0:T(8,128)(2,1)S(1)}) custom-call(s32[5]{0:T(128)S(1)} %stack.27.place, s32[64]{0:T(128)S(1)} %copy-done.6, bf16[1,2,512,1024]{3,2,1,0:T(8,128)(2,1)S(1)} %copy-done, bf16[1,2,512,1024]{3,2,1,0:T(8,128)(2,1)S(1)} %copy-done.2, ...), custom_call_target="tpu_custom_call" | custom-call | flops 805306368 | bytes 917504 | tf_op jit(solution)/shard_map/early_blocks/pallas_call | solution.py:28
  28.2 0.0 copy-start.1
  28.2 0.0 copy-start.3
  28.2 0.1 collective-permute-start.12
  28.3 0.0 collective-permute-done.7.incoming
  28.3 3.3 %early_blocks.3 = (bf16[256,1024]{1,0:T(8,128)(2,1)S(1)}, f32[2,256,128]{2,1,0:T(8,128)S(1)}, bf16[2,256,128]{2,1,0:T(8,128)(2,1)S(1)}) custom-call(s32[5]{0:T(128)S(1)} %stack.27.place, s32[64]{0:T(128)S(1)} %copy-done.6, bf16[1,2,512,1024]{3,2,1,0:T(8,128)(2,1)S(1)} %copy-done, bf16[1,2,512,1024]{3,2,1,0:T(8,128)(2,1)S(1)} %copy-done.2, ...), custom_call_target="tpu_custom_call" | custom-call | flops 805306368 | bytes 917504 | tf_op jit(solution)/shard_map/early_blocks/pallas_call | solution.py:28
  31.6 4.0 %collective-permute-start.8 = (bf16[2,256,128]{2,1,0:T(8,128)(2,1)S(1)}, bf16[2,256,128]{2,1,0:T(8,128)(2,1)S(1)}, u32[]{:S(2)}, u32[]{:S(2)}) collective-permute-start(bf16[2,256,128]{2,1,0:T(8,128)(2,1)S(1)} %get-tuple-element.49.d_local), channel_id=1, source_target_pairs={{4,8},{8,4},{12,16},{16,12},{20,24},{24,20},{5,9},{9,5},{13,17},{1... | collective-permute-start | bytes 393224 | tf_op jit(solution)/shard_map/ppermute | solution.py:198
  35.6 0.0 copy-done.1
  35.6 0.0 copy-done.3
  35.6 2.6 %late_blocks.3 = (bf16[256,1024]{1,0:T(8,128)(2,1)S(1)}, f32[2,512,128]{2,1,0:T(8,128)S(1)}) custom-call(s32[5]{0:T(128)S(1)} %stack.27.place, s32[64]{0:T(128)S(1)} %copy-done.6, bf16[1,2,512,1024]{3,2,1,0:T(8,128)(2,1)S(1)} %copy-done.1, bf16[1,2,512,1024]{3,2,1,0:T(8,128)(2,1)S(1)} %copy-done.3, bf16[2,512,128]{2,1,0:T(8,128)(2,1)S(1)} %get-tuple-element.40.other.keys), custom_call_target="tpu_custom_call" | custom-call | flops 805306368 | bytes 1048576 | tf_op jit(solution)/shard_map/late_blocks/pallas_call | solution.py:28
  38.2 0.0 collective-permute-done.12.d_back
  38.2 0.6 %pack_grads.3 = (bf16[2,128,128]{2,1,0:T(8,128)(2,1)S(1)}, bf16[2,128,128]{2,1,0:T(8,128)(2,1)S(1)}, bf16[2,128,128]{2,1,0:T(8,128)(2,1)S(1)}, bf16[2,128,128]{2,1,0:T(8,128)(2,1)S(1)}) custom-call(s32[5]{0:T(128)S(1)} %stack.27.place, f32[2,512,128]{2,1,0:T(8,128)S(1)} %get-tuple-element.54.d_late, f32[2,256,128]{2,1,0:T(8,128)S(1)} %get-tuple-element.55.d_own, ...), custom_call_target="tpu_custom_call" | custom-call | bytes 262144 | tf_op jit(solution)/shard_map/pack_grads/pallas_call | solution.py:28
  38.8 1.3 %collective-permute-start.13 = (bf16[2,128,128]{2,1,0:T(8,128)(2,1)S(1)}, bf16[2,128,128]{2,1,0:T(8,128)(2,1)S(1)}, u32[]{:S(2)}, u32[]{:S(2)}) collective-permute-start(bf16[2,128,128]{2,1,0:T(8,128)(2,1)S(1)} %get-tuple-element.58), channel_id=1, source_target_pairs={{0,1},{1,0},{2,3},{3,2},{4,5},{5,4},{6,7},{7,6},{8,9},{9,8},{10,11... | collective-permute-start | bytes 196616 | tf_op jit(solution)/shard_map/ppermute | solution.py:195
  40.1 2.8 %late_blocks.2 = (bf16[256,1024]{1,0:T(8,128)(2,1)S(1)}, f32[2,512,128]{2,1,0:T(8,128)S(1)}) custom-call(s32[5]{0:T(128)S(1)} %stack.27.place, s32[64]{0:T(128)S(1)} %copy-done.6, bf16[1,2,512,1024]{3,2,1,0:T(8,128)(2,1)S(1)} %copy-done.1, bf16[1,2,512,1024]{3,2,1,0:T(8,128)(2,1)S(1)} %copy-done.3, bf16[2,512,128]{2,1,0:T(8,128)(2,1)S(1)} %get-tuple-element.36.keys.other), custom_call_target="tpu_custom_call" | custom-call | flops 805306368 | bytes 1048576 | tf_op jit(solution)/shard_map/late_blocks/pallas_call | solution.py:28
  42.9 1.0 %collective-permute-start.14 = (bf16[2,128,128]{2,1,0:T(8,128)(2,1)S(1)}, bf16[2,128,128]{2,1,0:T(8,128)(2,1)S(1)}, u32[]{:S(2)}, u32[]{:S(2)}) collective-permute-start(bf16[2,128,128]{2,1,0:T(8,128)(2,1)S(1)} %get-tuple-element.59), channel_id=1, source_target_pairs={{0,2},{1,3},{2,0},{3,1},{4,6},{5,7},{6,4},{7,5},{8,10},{9,11},{10,... | collective-permute-start | bytes 196616 | tf_op jit(solution)/shard_map/ppermute | solution.py:195
  43.9 0.7 %collective-permute-start.15 = (bf16[2,128,128]{2,1,0:T(8,128)(2,1)S(1)}, bf16[2,128,128]{2,1,0:T(8,128)(2,1)S(1)}, u32[]{:S(2)}, u32[]{:S(2)}) collective-permute-start(bf16[2,128,128]{2,1,0:T(8,128)(2,1)S(1)} %get-tuple-element.60), channel_id=1, source_target_pairs={{0,3},{1,2},{2,1},{3,0},{4,7},{5,6},{6,5},{7,4},{8,11},{9,10},{10,... | collective-permute-start | bytes 196616 | tf_op jit(solution)/shard_map/ppermute | solution.py:195
  44.6 0.0 collective-permute-done.8.d_back
  44.6 0.6 %pack_grads.2 = (bf16[2,128,128]{2,1,0:T(8,128)(2,1)S(1)}, bf16[2,128,128]{2,1,0:T(8,128)(2,1)S(1)}, bf16[2,128,128]{2,1,0:T(8,128)(2,1)S(1)}, bf16[2,128,128]{2,1,0:T(8,128)(2,1)S(1)}) custom-call(s32[5]{0:T(128)S(1)} %stack.27.place, f32[2,512,128]{2,1,0:T(8,128)S(1)} %get-tuple-element.47.d_late, f32[2,256,128]{2,1,0:T(8,128)S(1)} %get-tuple-element.48.d_own, ...), custom_call_target="tpu_custom_call" | custom-call | bytes 262144 | tf_op jit(solution)/shard_map/pack_grads/pallas_call | solution.py:28
  45.3 1.0 %collective-permute-start.10 = (bf16[2,128,128]{2,1,0:T(8,128)(2,1)S(1)}, bf16[2,128,128]{2,1,0:T(8,128)(2,1)S(1)}, u32[]{:S(2)}, u32[]{:S(2)}) collective-permute-start(bf16[2,128,128]{2,1,0:T(8,128)(2,1)S(1)} %get-tuple-element.52), channel_id=1, source_target_pairs={{0,2},{1,3},{2,0},{3,1},{4,6},{5,7},{6,4},{7,5},{8,10},{9,11},{10,... | collective-permute-start | bytes 196616 | tf_op jit(solution)/shard_map/ppermute | solution.py:195
  46.3 0.9 %collective-permute-start.11 = (bf16[2,128,128]{2,1,0:T(8,128)(2,1)S(1)}, bf16[2,128,128]{2,1,0:T(8,128)(2,1)S(1)}, u32[]{:S(2)}, u32[]{:S(2)}) collective-permute-start(bf16[2,128,128]{2,1,0:T(8,128)(2,1)S(1)} %get-tuple-element.53), channel_id=1, source_target_pairs={{0,3},{1,2},{2,1},{3,0},{4,7},{5,6},{6,5},{7,4},{8,11},{9,10},{10,... | collective-permute-start | bytes 196616 | tf_op jit(solution)/shard_map/ppermute | solution.py:195
  47.2 0.0 collective-permute-done.13.refs_5_
  47.2 0.0 collective-permute-start.9
  47.2 1.9 %store_queries.1 = bf16[1,2,512,1024]{3,2,1,0:T(8,128)(2,1)} custom-call(s32[5]{0:T(128)S(1)} %stack.27.place, bf16[256,1024]{1,0:T(8,128)(2,1)S(1)} %get-tuple-element.42.early_first, bf16[256,1024]{1,0:T(8,128)(2,1)S(1)} %get-tuple-element.43.late_first, bf16[256,1024]{1,0:T(8,128)(2,1)S(1)} %get-tuple-element.45.early_second, ...), custom_call_target="tpu_custom_call" | custom-call | bytes 2097152 | tf_op jit(solution)/shard_map/store_queries/pallas_call | solution.py:28
  49.1 0.0 collective-permute-done.14.refs_6_
  49.1 0.0 collective-permute-done.15.refs_7_
  49.1 0.4 collective-permute-done.10.refs_2_
  49.6 1.5 %collective-permute-done.11.refs_3_ = bf16[2,128,128]{2,1,0:T(8,128)(2,1)S(1)} collective-permute-done((bf16[2,128,128]{2,1,0:T(8,128)(2,1)S(1)}, bf16[2,128,128]{2,1,0:T(8,128)(2,1)S(1)}, u32[]{:S(2)}, u32[]{:S(2)}) %collective-permute-start.11) | collective-permute-done | bytes 65568 | tf_op jit(solution)/shard_map/ppermute | solution.py:195
  51.0 0.0 collective-permute-done.9.refs_1_
  51.0 1.4 %join_grads.1 = (bf16[1,2,128,512]{3,2,1,0:T(8,128)(2,1)}, bf16[1,2,128,512]{3,2,1,0:T(8,128)(2,1)}) custom-call(s32[5]{0:T(128)S(1)} %stack.27.place, bf16[2,128,128]{2,1,0:T(8,128)(2,1)S(1)} %get-tuple-element.50.refs_0_, bf16[2,128,128]{2,1,0:T(8,128)(2,1)S(1)} %collective-permute-done.9.refs_1_, ...), custom_call_target="tpu_custom_call" | custom-call | bytes 524288 | tf_op jit(solution)/shard_map/join_grads/pallas_call | solution.py:28
Async XLA Ops:
  0.7 1.0 %copy-start.4 = (bf16[1,2,128,512]{3,2,1,0:T(8,128)(2,1)S(1)}, bf16[1,2,128,512]{3,2,1,0:T(8,128)(2,1)}, u32[]{:S(2)}) copy-start(bf16[1,2,128,512]{3,2,1,0:T(8,128)(2,1)} %key.5) | copy-start | bytes 786436
  1.7 0.9 %copy-start.5 = (bf16[1,2,128,512]{3,2,1,0:T(8,128)(2,1)S(1)}, bf16[1,2,128,512]{3,2,1,0:T(8,128)(2,1)}, u32[]{:S(2)}) copy-start(bf16[1,2,128,512]{3,2,1,0:T(8,128)(2,1)} %value.5) | copy-start | bytes 786436
  3.3 2.5 %collective-permute-start.3 = (bf16[2,128,128]{2,1,0:T(8,128)(2,1)S(1)}, bf16[2,128,128]{2,1,0:T(8,128)(2,1)S(1)}, u32[]{:S(2)}, u32[]{:S(2)}) collective-permute-start(bf16[2,128,128]{2,1,0:T(8,128)(2,1)S(1)} %get-tuple-element.37), channel_id=1, source_target_pairs={{0,1},{1,0},{2,3},{3,2},{4,5},{5,4},{6,7},{7,6},{8,9},{9,8},{10,11... | collective-permute-start | bytes 196616 | tf_op jit(solution)/shard_map/ppermute | solution.py:195
  4.0 3.7 %collective-permute-start.4 = (bf16[2,128,128]{2,1,0:T(8,128)(2,1)S(1)}, bf16[2,128,128]{2,1,0:T(8,128)(2,1)S(1)}, u32[]{:S(2)}, u32[]{:S(2)}) collective-permute-start(bf16[2,128,128]{2,1,0:T(8,128)(2,1)S(1)} %get-tuple-element.38), channel_id=1, source_target_pairs={{0,2},{1,3},{2,0},{3,1},{4,6},{5,7},{6,4},{7,5},{8,10},{9,11},{10,... | collective-permute-start | bytes 196616 | tf_op jit(solution)/shard_map/ppermute | solution.py:195
  5.2 4.0 %collective-permute-start.5 = (bf16[2,128,128]{2,1,0:T(8,128)(2,1)S(1)}, bf16[2,128,128]{2,1,0:T(8,128)(2,1)S(1)}, u32[]{:S(2)}, u32[]{:S(2)}) collective-permute-start(bf16[2,128,128]{2,1,0:T(8,128)(2,1)S(1)} %get-tuple-element.39), channel_id=1, source_target_pairs={{0,3},{1,2},{2,1},{3,0},{4,7},{5,6},{6,5},{7,4},{8,11},{9,10},{10,... | collective-permute-start | bytes 196616 | tf_op jit(solution)/shard_map/ppermute | solution.py:195
  9.9 11.0 %collective-permute-start.6 = (bf16[2,256,128]{2,1,0:T(8,128)(2,1)S(1)}, bf16[2,256,128]{2,1,0:T(8,128)(2,1)S(1)}, u32[]{:S(2)}, u32[]{:S(2)}) collective-permute-start(bf16[2,256,128]{2,1,0:T(8,128)(2,1)S(1)} %get-tuple-element.41), channel_id=1, source_target_pairs={{0,4},{4,0},{8,12},{12,8},{16,20},{20,16},{24,28},{28,24},{1,5},{5... | collective-permute-start | bytes 393224 | tf_op jit(solution)/shard_map/ppermute | solution.py:199
  10.2 2.3 %collective-permute-start = (bf16[2,128,128]{2,1,0:T(8,128)(2,1)S(1)}, bf16[2,128,128]{2,1,0:T(8,128)(2,1)S(1)}, u32[]{:S(2)}, u32[]{:S(2)}) collective-permute-start(bf16[2,128,128]{2,1,0:T(8,128)(2,1)S(1)} %get-tuple-element.33), channel_id=1, source_target_pairs={{0,1},{1,0},{2,3},{3,2},{4,5},{5,4},{6,7},{7,6},{8,9},{9,8},{10,11... | collective-permute-start | bytes 196616 | tf_op jit(solution)/shard_map/ppermute | solution.py:195
  10.8 3.7 %collective-permute-start.1 = (bf16[2,128,128]{2,1,0:T(8,128)(2,1)S(1)}, bf16[2,128,128]{2,1,0:T(8,128)(2,1)S(1)}, u32[]{:S(2)}, u32[]{:S(2)}) collective-permute-start(bf16[2,128,128]{2,1,0:T(8,128)(2,1)S(1)} %get-tuple-element.34), channel_id=1, source_target_pairs={{0,2},{1,3},{2,0},{3,1},{4,6},{5,7},{6,4},{7,5},{8,10},{9,11},{10,... | collective-permute-start | bytes 196616 | tf_op jit(solution)/shard_map/ppermute | solution.py:195
  11.8 4.2 %collective-permute-start.2 = (bf16[2,128,128]{2,1,0:T(8,128)(2,1)S(1)}, bf16[2,128,128]{2,1,0:T(8,128)(2,1)S(1)}, u32[]{:S(2)}, u32[]{:S(2)}) collective-permute-start(bf16[2,128,128]{2,1,0:T(8,128)(2,1)S(1)} %get-tuple-element.35), channel_id=1, source_target_pairs={{0,3},{1,2},{2,1},{3,0},{4,7},{5,6},{6,5},{7,4},{8,11},{9,10},{10,... | collective-permute-start | bytes 196616 | tf_op jit(solution)/shard_map/ppermute | solution.py:195
  16.6 11.7 %collective-permute-start.7 = (bf16[2,256,128]{2,1,0:T(8,128)(2,1)S(1)}, bf16[2,256,128]{2,1,0:T(8,128)(2,1)S(1)}, u32[]{:S(2)}, u32[]{:S(2)}) collective-permute-start(bf16[2,256,128]{2,1,0:T(8,128)(2,1)S(1)} %get-tuple-element.44), channel_id=1, source_target_pairs={{4,8},{8,4},{12,16},{16,12},{20,24},{24,20},{5,9},{9,5},{13,17},{1... | collective-permute-start | bytes 393224 | tf_op jit(solution)/shard_map/ppermute | solution.py:198
  20.8 1.6 %copy-start = (bf16[1,2,512,1024]{3,2,1,0:T(8,128)(2,1)S(1)}, bf16[1,2,512,1024]{3,2,1,0:T(8,128)(2,1)}, u32[]{:S(2)}) copy-start(bf16[1,2,512,1024]{3,2,1,0:T(8,128)(2,1)} %query.7) | copy-start | bytes 6291460
  22.4 1.6 %copy-start.2 = (bf16[1,2,512,1024]{3,2,1,0:T(8,128)(2,1)S(1)}, bf16[1,2,512,1024]{3,2,1,0:T(8,128)(2,1)}, u32[]{:S(2)}) copy-start(bf16[1,2,512,1024]{3,2,1,0:T(8,128)(2,1)} %d_out.7) | copy-start | bytes 6291460
  24.0 0.7 %copy-start.6 = (s32[64]{0:T(128)S(1)}, s32[64]{0:T(128)}, u32[]{:S(2)}) copy-start(s32[64]{0:T(128)} %doc_start.7) | copy-start | bytes 772
  28.2 7.4 %copy-start.1 = (bf16[1,2,512,1024]{3,2,1,0:T(8,128)(2,1)S(1)}, bf16[1,2,512,1024]{3,2,1,0:T(8,128)(2,1)}, u32[]{:S(2)}) copy-start(bf16[1,2,512,1024]{3,2,1,0:T(8,128)(2,1)} %query.7) | copy-start | bytes 6291460
  28.2 7.4 %copy-start.3 = (bf16[1,2,512,1024]{3,2,1,0:T(8,128)(2,1)S(1)}, bf16[1,2,512,1024]{3,2,1,0:T(8,128)(2,1)}, u32[]{:S(2)}) copy-start(bf16[1,2,512,1024]{3,2,1,0:T(8,128)(2,1)} %d_out.7) | copy-start | bytes 6291460
  28.2 10.0 %collective-permute-start.12 = (bf16[2,256,128]{2,1,0:T(8,128)(2,1)S(1)}, bf16[2,256,128]{2,1,0:T(8,128)(2,1)S(1)}, u32[]{:S(2)}, u32[]{:S(2)}) collective-permute-start(bf16[2,256,128]{2,1,0:T(8,128)(2,1)S(1)} %get-tuple-element.56.d_local), channel_id=1, source_target_pairs={{0,4},{4,0},{8,12},{12,8},{16,20},{20,16},{24,28},{28,24},{1,5},{5... | collective-permute-start | bytes 393224 | tf_op jit(solution)/shard_map/ppermute | solution.py:199
  31.6 13.0 %collective-permute-start.8 = (bf16[2,256,128]{2,1,0:T(8,128)(2,1)S(1)}, bf16[2,256,128]{2,1,0:T(8,128)(2,1)S(1)}, u32[]{:S(2)}, u32[]{:S(2)}) collective-permute-start(bf16[2,256,128]{2,1,0:T(8,128)(2,1)S(1)} %get-tuple-element.49.d_local), channel_id=1, source_target_pairs={{4,8},{8,4},{12,16},{16,12},{20,24},{24,20},{5,9},{9,5},{13,17},{1... | collective-permute-start | bytes 393224 | tf_op jit(solution)/shard_map/ppermute | solution.py:198
  38.8 8.3 %collective-permute-start.13 = (bf16[2,128,128]{2,1,0:T(8,128)(2,1)S(1)}, bf16[2,128,128]{2,1,0:T(8,128)(2,1)S(1)}, u32[]{:S(2)}, u32[]{:S(2)}) collective-permute-start(bf16[2,128,128]{2,1,0:T(8,128)(2,1)S(1)} %get-tuple-element.58), channel_id=1, source_target_pairs={{0,1},{1,0},{2,3},{3,2},{4,5},{5,4},{6,7},{7,6},{8,9},{9,8},{10,11... | collective-permute-start | bytes 196616 | tf_op jit(solution)/shard_map/ppermute | solution.py:195
  42.9 6.2 %collective-permute-start.14 = (bf16[2,128,128]{2,1,0:T(8,128)(2,1)S(1)}, bf16[2,128,128]{2,1,0:T(8,128)(2,1)S(1)}, u32[]{:S(2)}, u32[]{:S(2)}) collective-permute-start(bf16[2,128,128]{2,1,0:T(8,128)(2,1)S(1)} %get-tuple-element.59), channel_id=1, source_target_pairs={{0,2},{1,3},{2,0},{3,1},{4,6},{5,7},{6,4},{7,5},{8,10},{9,11},{10,... | collective-permute-start | bytes 196616 | tf_op jit(solution)/shard_map/ppermute | solution.py:195
  43.9 5.2 %collective-permute-start.15 = (bf16[2,128,128]{2,1,0:T(8,128)(2,1)S(1)}, bf16[2,128,128]{2,1,0:T(8,128)(2,1)S(1)}, u32[]{:S(2)}, u32[]{:S(2)}) collective-permute-start(bf16[2,128,128]{2,1,0:T(8,128)(2,1)S(1)} %get-tuple-element.60), channel_id=1, source_target_pairs={{0,3},{1,2},{2,1},{3,0},{4,7},{5,6},{6,5},{7,4},{8,11},{9,10},{10,... | collective-permute-start | bytes 196616 | tf_op jit(solution)/shard_map/ppermute | solution.py:195
  45.3 4.3 %collective-permute-start.10 = (bf16[2,128,128]{2,1,0:T(8,128)(2,1)S(1)}, bf16[2,128,128]{2,1,0:T(8,128)(2,1)S(1)}, u32[]{:S(2)}, u32[]{:S(2)}) collective-permute-start(bf16[2,128,128]{2,1,0:T(8,128)(2,1)S(1)} %get-tuple-element.52), channel_id=1, source_target_pairs={{0,2},{1,3},{2,0},{3,1},{4,6},{5,7},{6,4},{7,5},{8,10},{9,11},{10,... | collective-permute-start | bytes 196616 | tf_op jit(solution)/shard_map/ppermute | solution.py:195
  46.3 4.8 %collective-permute-start.11 = (bf16[2,128,128]{2,1,0:T(8,128)(2,1)S(1)}, bf16[2,128,128]{2,1,0:T(8,128)(2,1)S(1)}, u32[]{:S(2)}, u32[]{:S(2)}) collective-permute-start(bf16[2,128,128]{2,1,0:T(8,128)(2,1)S(1)} %get-tuple-element.53), channel_id=1, source_target_pairs={{0,3},{1,2},{2,1},{3,0},{4,7},{5,6},{6,5},{7,4},{8,11},{9,10},{10,... | collective-permute-start | bytes 196616 | tf_op jit(solution)/shard_map/ppermute | solution.py:195
  47.2 3.8 %collective-permute-start.9 = (bf16[2,128,128]{2,1,0:T(8,128)(2,1)S(1)}, bf16[2,128,128]{2,1,0:T(8,128)(2,1)S(1)}, u32[]{:S(2)}, u32[]{:S(2)}) collective-permute-start(bf16[2,128,128]{2,1,0:T(8,128)(2,1)S(1)} %get-tuple-element.51), channel_id=1, source_target_pairs={{0,1},{1,0},{2,3},{3,2},{4,5},{5,4},{6,7},{7,6},{8,9},{9,8},{10,11... | collective-permute-start | bytes 196616 | tf_op jit(solution)/shard_map/ppermute | solution.py:195

commit v2 on v1

v2 whole, which is shorter than its diff:
```python
import functools

import jax
import jax.numpy as jnp
from jax import lax
from jax.experimental import pallas as pl
from jax.experimental.pallas import tpu as pltpu
from jax.sharding import PartitionSpec as P

HD = 128
BLK = 128
REACH = 2
SCALE = HD**-0.5
SCALE_LOG2E = SCALE * 1.4426950408889634
BF16 = jnp.bfloat16
F32 = jnp.float32
VMEM = pl.BlockSpec(memory_space=pltpu.VMEM)
HBM = pl.BlockSpec(memory_space=pltpu.HBM)
ANY = pl.BlockSpec(memory_space=pl.ANY)
SMEM = pl.BlockSpec(memory_space=pltpu.SMEM)


def shape(dims, dtype=BF16):
    return jax.ShapeDtypeStruct(dims, dtype)


def call(body, inputs, outs, scratch=(), flops=0, moved=0, limit=12, far=(), after=(), out_spec=VMEM):
    in_specs = [ANY] * len(after) + [
        SMEM if a.dtype == jnp.int32 else HBM if i in far else VMEM for i, a in enumerate(inputs)
    ]
    skip = len(after)
    name = body.func.__name__
    return pl.pallas_call(
        lambda *refs: body(*refs[skip:]),
        out_shape=outs,
        in_specs=in_specs,
        out_specs=[out_spec] * len(outs),
        scratch_shapes=list(scratch),
        compiler_params=pltpu.CompilerParams(vmem_limit_bytes=limit << 20),
        cost_estimate=pl.CostEstimate(flops=flops, bytes_accessed=moved, transcendentals=0),
        name=name,
    )(*after, *inputs)


def carry(pairs, sems):
    copies = [pltpu.make_async_copy(a, b, sems.at[i]) for i, (a, b) in enumerate(pairs)]
    for copy in copies:
        copy.start()
    for copy in copies:
        copy.wait()


def lanes(index):
    return pl.ds(pl.multiple_of(index * HD, HD), HD)


def rows(index, blocks=1):
    return pl.ds(pl.multiple_of(index * BLK, BLK), blocks * BLK)


def slot_of(place, half):
    return place[1] if half == 0 else 1 - place[1]


def pack_keys(heads, place, key, value, *refs):
    own, near, sends, sems = refs[0], refs[1], refs[2:-1], refs[-1]
    me = place[0]
    pairs = []
    for half in range(2):
        for t in range(heads):
            there = own.at[half] if t == 0 else near.at[half] if t == 1 else sends[half * (heads - 2) + t - 2]
            for i, array in enumerate((key, value)):
                pairs.append((array.at[0, slot_of(place, half), :, lanes(me ^ t)], there.at[i]))
    carry(pairs, sems)


def load_queries(doc_start, query, d_out, query_near, d_out_near, sems):
    carry([(query, query_near), (d_out, d_out_near)], sems)


def join_keys(heads, half, place, own, near, *refs):
    parts, (span, rim) = refs[: heads - 2], refs[heads - 2 :]
    me = place[0]
    for t in range(heads):
        part = own.at[half] if t == 0 else near.at[half] if t == 1 else parts[t - 2]
        span[0, rows(me ^ t), :] = part[0]
        span[1, rows(me ^ t), :] = part[1]
    rim[...] = span[:, (heads - REACH) * BLK :, :]


def dot(a, b, ca, cb):
    return lax.dot_general(a, b, (((ca,), (cb,)), ((), ())), preferred_element_type=F32)


def block_grads(n, first, queries, grads, keys, d_queries, d_keys):
    count = queries.shape[1] // HD
    window = pl.ds(first * BLK, n * BLK)
    k, v = keys[0, window, :], keys[1, window, :]
    q = jnp.concatenate([queries[:, j * HD : (j + 1) * HD] for j in range(count)], axis=0)
    do = jnp.concatenate([grads[:, j * HD : (j + 1) * HD] for j in range(count)], axis=0)
    s = dot(k, q, 1, 1)
    dp = dot(v, do, 1, 1)
    token = lax.broadcasted_iota(jnp.int32, (BLK, count * BLK), 1) & (BLK - 1)
    seen = lax.broadcasted_iota(jnp.int32, (BLK, count * BLK), 0) <= token
    last = jnp.where(seen, s[(n - 1) * BLK :], -jnp.inf)
    s = jnp.concatenate([s[: (n - 1) * BLK], last], axis=0) if n > 1 else last
    peak = jnp.max(s, axis=0, keepdims=True)
    w = jnp.exp2((s - peak) * SCALE_LOG2E)
    inverse = 1.0 / jnp.sum(w, axis=0, keepdims=True)
    delta = jnp.sum(w * dp, axis=0, keepdims=True) * inverse
    p = w * inverse
    ds = (p * (dp - delta)).astype(BF16)
    d_keys[0, window, :] += dot(ds, q, 1, 0) * SCALE
    d_keys[1, window, :] += dot(p.astype(BF16), do, 1, 0)
    dq = (dot(k.T, ds, 1, 0) * SCALE).astype(BF16)
    for j in range(count):
        d_queries[:, j * HD : (j + 1) * HD] = dq[:, j * BLK : (j + 1) * BLK].T


def span_part(first_block, blocks, per_span, half, place, doc_start, query, d_out, keys, d_query, d_keys):
    slot = slot_of(place, half)
    d_keys[...] = jnp.zeros_like(d_keys)
    for b in range(blocks):
        block = place[3 + slot] * per_span + first_block + b
        before = doc_start[jnp.maximum(block - 1, 0)]
        visible = jnp.where(doc_start[block] == 1, 1, jnp.where(before == 1, 2, 3))
        tokens = pl.ds((first_block + b) * BLK, BLK)
        for n in range(1, REACH + 2):

            @pl.when(visible == n)
            def _(n=n, tokens=tokens, b=b):
                block_grads(
                    n,
                    b + REACH + 1 - n,
                    query.at[0, slot, tokens, :],
                    d_out.at[0, slot, tokens, :],
                    keys,
                    d_query.at[pl.ds(b * BLK, BLK), :],
                    d_keys,
                )


def late_blocks(per_span, half, place, doc_start, query, d_out, keys, d_query, d_keys):
    span_part(REACH, per_span - REACH, per_span, half, place, doc_start, query, d_out, keys, d_query, d_keys)


def early_blocks(per_span, half, place, doc_start, query, d_out, keys, other, incoming, d_query, d_own, d_rim, window, d_window):
    cut = REACH * BLK
    window[:, cut:, :] = keys[:, :cut, :]
    window[:, :cut, :] = incoming[...]
    if half == 1:

        @pl.when(place[2] == 1)
        def _():
            window[:, :cut, :] = other[:, (per_span - REACH) * BLK :, :]

    span_part(0, REACH, per_span, half, place, doc_start, query, d_out, window, d_query, d_window)
    d_rim[...] = d_window[:, :cut, :].astype(BF16)
    d_own[...] = d_window[:, cut:, :]


def store_queries(reach, place, early_first, late_first, early_second, late_second, d_query, sems):
    pairs = []
    for half, parts in ((0, (early_first, late_first)), (1, (early_second, late_second))):
        for part, start in zip(parts, (0, reach * BLK)):
            pairs.append((part, d_query.at[0, slot_of(place, half), pl.ds(start, part.shape[0]), :]))
    carry(pairs, sems)


def pack_grads(heads, place, late_0, own_0, back_0, edge_0, late_1, own_1, back_1, edge_1, *refs):
    sends, total = refs[:-1], refs[-1]
    me = place[0]
    cut = REACH * BLK
    for half, (late, own, back) in enumerate(((late_0, own_0, back_0), (late_1, own_1, back_1))):
        total[...] = late[...]
        total[:, :cut, :] += own[...]
        total[:, (heads - REACH) * BLK :, :] += back[...].astype(F32)
        if half == 0:

            @pl.when(place[2] == 1)
            def _():
                total[:, (heads - REACH) * BLK :, :] += edge_1[...].astype(F32)

        for t in range(heads):
            sends[t][half] = total[:, rows(me ^ t), :].astype(BF16)


def join_grads(heads, place, *refs):
    parts, (d_key, d_value, sems) = refs[:heads], refs[heads:]
    me = place[0]
    pairs = []
    for t in range(heads):
        for half in range(2):
            for i, array in enumerate((d_key, d_value)):
                pairs.append(
                    (parts[t].at[half, i], array.at[0, slot_of(place, half), :, lanes(me ^ t)])
                )
    carry(pairs, sems)


def per_device(query, key, value, d_out, doc_start):
    ctx, ctx_count = lax.axis_index("ctx"), lax.axis_size("ctx")
    head, heads = lax.axis_index("head"), lax.axis_size("head")
    odd = ctx % 2
    first = 1 - odd
    is_last = (ctx == ctx_count - 1).astype(jnp.int32)
    place = jnp.stack([head, first, is_last, ctx, 2 * ctx_count - 1 - ctx]).astype(jnp.int32)
    block = shape((2, BLK, HD))
    partners = range(1, heads)
    swap = lambda x, t: lax.ppermute(x, "head", [(i, i ^ t) for i in range(heads)])
    outer = [p for i in range(1, ctx_count - 1, 2) for p in ((i, i + 1), (i + 1, i))]
    inner = [p for i in range(0, ctx_count, 2) for p in ((i, i + 1), (i + 1, i))]
    to_outer = lambda x: lax.ppermute(x, "ctx", outer)
    to_inner = lambda x: lax.ppermute(x, "ctx", inner)

    key, value, query, d_out = (
        pltpu.with_memory_space_constraint(x, pltpu.HBM) for x in (key, value, query, d_out)
    )
    own, near, *sends = call(
        functools.partial(pack_keys, heads),
        (place, key, value),
        [shape((2, 2, BLK, HD))] * 2 + [block] * (2 * (heads - 2)),
        scratch=[pltpu.SemaphoreType.DMA((4 * heads,))],
        far=(1, 2),
    )
    near = swap(near, 1)
    parts = [
        [swap(sends[half * (heads - 2) + t - 2], t) for t in range(2, heads)] for half in range(2)
    ]
    query, d_out = call(
        functools.partial(load_queries),
        (doc_start, query, d_out),
        [shape(query.shape), shape(d_out.shape)],
        scratch=[pltpu.SemaphoreType.DMA((2,))],
        moved=4 * query.size,
        far=(1, 2),
        after=(own,),
    )
    joined = []
    for half in range(2):
        joined.append(
            call(
                functools.partial(join_keys, heads, half),
                (place, own, near, *parts[half]),
                [shape((2, heads * BLK, HD)), shape((2, REACH * BLK, HD))],
                after=(query,) if half == 0 else (joined[0][1],),
            )
        )
    keys = [j[0] for j in joined]
    rim_second = to_outer(joined[0][1])
    rim_first = to_inner(joined[1][1])
    flops = 8 * BLK * BLK * HD * (query.shape[3] // HD) * REACH * (REACH + 1)

    def late(half, after):
        return call(
            functools.partial(late_blocks, heads, half),
            (place, doc_start, query, d_out, keys[half]),
            [shape(((heads - REACH) * BLK, query.shape[3])), shape((2, heads * BLK, HD), F32)],
            flops=flops,
            limit=20,
            after=after,
        )

    def early(half, incoming, after):
        return call(
            functools.partial(early_blocks, heads, half),
            (place, doc_start, query, d_out, keys[half], keys[1 - half], incoming),
            [
                shape((REACH * BLK, query.shape[3])),
                shape((2, REACH * BLK, HD), F32),
                shape((2, REACH * BLK, HD)),
            ],
            scratch=[
                pltpu.VMEM((2, 2 * REACH * BLK, HD), BF16),
                pltpu.VMEM((2, 2 * REACH * BLK, HD), F32),
            ],
            flops=flops,
            limit=20,
            after=after,
        )

    dq_late_first, late_first = late(0, (joined[1][1],))
    dq_early_second, own_second, edge_second = early(1, rim_second, (late_first,))
    back_first = to_outer(edge_second)
    dq_early_first, own_first, edge_first = early(0, rim_first, (edge_second,))
    back_second = to_inner(edge_first)
    dq_late_second, late_second = late(1, (edge_first,))
    d_query = call(
        functools.partial(store_queries, REACH),
        (place, dq_early_first, dq_late_first, dq_early_second, dq_late_second),
        [shape(query.shape)],
        scratch=[pltpu.SemaphoreType.DMA((4,))],
        out_spec=ANY,
    )[0]

    grads = call(
        functools.partial(pack_grads, heads),
        (place, late_first, own_first, back_first, edge_first)
        + (late_second, own_second, back_second, edge_second),
        [shape((2, 2, BLK, HD))] * heads,
        scratch=[pltpu.VMEM((2, heads * BLK, HD), F32)],
    )
    d_key, d_value = call(
        functools.partial(join_grads, heads),
        (place, grads[0], *[swap(grads[t], t) for t in partners]),
        [shape(key.shape), shape(value.shape)],
        scratch=[pltpu.SemaphoreType.DMA((4 * heads,))],
        out_spec=ANY,
    )
    return d_query, d_key, d_value


def solution(mesh):
    tokens = P("ctx", None, "head", None)
    columns = P("ctx", None, None, "head")
    return jax.shard_map(
        per_device,
        mesh=mesh,
        in_specs=(columns, tokens, tokens, columns, P()),
        out_specs=(columns, tokens, tokens),
        check_vma=False,
    )
```

time: 52.7 us -> 46.5 us (0.88)
  the two profiles are of different devices: /device:TPU:13 before, /device:TPU:0 now
where the time goes in v2:
time: 46.5 us; the launch traced here: 45.9 us
  Pallas kernels  21 us (45%)
  starting transfers between devices  18.2 us (39%)
  waiting for transfers between devices  4.93 us (11%)
  between operations  1.01 us (2%)
  local copies, waits for them, and re-layouts  0.75 us (2%)
    pallas_call x11, Pallas kernels, call(): pl.pallas_call(lambda *refs: body(*refs[skip:]), out_shape=outs, in_specs...  21 us
    ppermute x2, starting transfers between devices, per_device(): to_inner = lambda x: lax.ppermute(x, 'ctx', inner)  10 us
    ppermute x8, starting transfers between devices, per_device(): lax.ppermute(x, 'head', [(i, i ^ t) for i in range(heads)])  6.83 us
    ppermute x8, waiting for transfers between devices, per_device(): lax.ppermute(x, 'head', [(i, i ^ t) for i in range(heads)])  4.8 us
    ppermute x2, starting transfers between devices, per_device(): to_outer = lambda x: lax.ppermute(x, 'ctx', outer)  1.34 us
  transfers between devices with their start and end apart: 12, of which 4 were waited for; matrix products, arithmetic and copies ran while one was open for 0% of the time, Pallas kernels for 37%

profile of v2, /device:TPU:0, one launch (start us, length us, event | category | flops | bytes accessed | tf_op | source)
XLA Modules:
  0.0 45.9 jit_solution(4860514146345781650)
XLA Ops:
  0.6 0.1 stack.27.refs_0_.refs_1_
  0.7 1.7 %pack_keys.1 = (bf16[2,2,128,128]{3,2,1,0:T(8,128)(2,1)S(1)}, bf16[2,2,128,128]{3,2,1,0:T(8,128)(2,1)S(1)}, bf16[2,128,128]{2,1,0:T(8,128)(2,1)S(1)}, bf16[2,128...) custom-call(s32[5]{0:T(128)S(1)} %stack.27.refs_0_.refs_1_, ...), custom_call_target="tpu_custom_call" | custom-call | tf_op jit(solution)/shard_map/pack_keys/pallas_call | solution.py:33
  2.4 0.5 %collective-permute-start = (bf16[2,2,128,128]{3,2,1,0:T(8,128)(2,1)S(1)}, bf16[2,2,128,128]{3,2,1,0:T(8,128)(2,1)S(1)}, u32[]{:S(2)}, u32[]{:S(2)}) collective-permute-start(bf16[2,2,128,128]{3,2,1,0:T(8,128)(2,1)S(1)} %get-tuple-element.33), channel_id=1, source_target_pairs={{0,1},{1,0},{2,3},{3,2},{4,5},{5,4},{6,7},{7,6},{8,9},{9,8},{10,11... | collective-permute-start | bytes 393224 | tf_op jit(solution)/shard_map/ppermute | solution.py:210
  3.0 2.6 %collective-permute-start.1 = (bf16[2,128,128]{2,1,0:T(8,128)(2,1)S(1)}, bf16[2,128,128]{2,1,0:T(8,128)(2,1)S(1)}, u32[]{:S(2)}, u32[]{:S(2)}) collective-permute-start(bf16[2,128,128]{2,1,0:T(8,128)(2,1)S(1)} %get-tuple-element.34), channel_id=1, source_target_pairs={{0,2},{1,3},{2,0},{3,1},{4,6},{5,7},{6,4},{7,5},{8,10},{9,11},{10,... | collective-permute-start | bytes 196616 | tf_op jit(solution)/shard_map/ppermute | solution.py:210
  5.5 0.1 collective-permute-start.2
  5.6 1.7 %collective-permute-start.3 = (bf16[2,128,128]{2,1,0:T(8,128)(2,1)S(1)}, bf16[2,128,128]{2,1,0:T(8,128)(2,1)S(1)}, u32[]{:S(2)}, u32[]{:S(2)}) collective-permute-start(bf16[2,128,128]{2,1,0:T(8,128)(2,1)S(1)} %get-tuple-element.37), channel_id=1, source_target_pairs={{0,2},{1,3},{2,0},{3,1},{4,6},{5,7},{6,4},{7,5},{8,10},{9,11},{10,... | collective-permute-start | bytes 196616 | tf_op jit(solution)/shard_map/ppermute | solution.py:210
  7.3 0.0 collective-permute-start.4
  7.3 0.0 copy-start
  7.3 0.7 %copy-done = s32[64]{0:T(128)S(1)} copy-done((s32[64]{0:T(128)S(1)}, s32[64]{0:T(128)}, u32[]{:S(2)}) %copy-start) | copy-done | bytes 280
  8.0 2.8 %load_queries.1 = (bf16[1,2,512,1024]{3,2,1,0:T(8,128)(2,1)S(1)}, bf16[1,2,512,1024]{3,2,1,0:T(8,128)(2,1)S(1)}) custom-call(bf16[2,2,128,128]{3,2,1,0:T(8,128)(2,1)S(1)} %get-tuple-element.31.refs_0_.refs_2_, s32[64]{0:T(128)S(1)} %copy-done, bf16[1,2,512,1024]{3,2,1,0:T(8,128)(2,1)} %refs_2_.7, bf16[1,2,512,1024]{3,2,1,0:T(8,128)(2,1)} %refs_3_.1), custom_call_target="tpu_custom_call" | custom-call | bytes 4194304 | tf_op jit(solution)/shard_map/load_queries/pallas_call | solution.py:33
  10.8 0.0 copy-start.1
  10.8 0.0 collective-permute-done.1.refs_4_
  10.8 0.0 collective-permute-done.2.refs_5_
  10.8 0.0 collective-permute-done.refs_3_
  10.8 0.6 %join_keys.2 = (bf16[2,512,128]{2,1,0:T(8,128)(2,1)S(1)}, bf16[2,256,128]{2,1,0:T(8,128)(2,1)S(1)}) custom-call(bf16[1,2,512,1024]{3,2,1,0:T(8,128)(2,1)S(1)} %get-tuple-element.32.refs_0_.refs_3_, s32[5]{0:T(128)S(1)} %stack.27.refs_0_.refs_1_, bf16[2,2,128,128]{3,2,1,0:T(8,128)(2,1)S(1)} %get-tuple-element.31.refs_0_.refs_2_, ...), custom_call_target="tpu_custom_call" | custom-call | tf_op jit(solution)/shard_map/join_keys/pallas_call | solution.py:33
  11.4 0.7 %collective-permute-start.5 = (bf16[2,256,128]{2,1,0:T(8,128)(2,1)S(1)}, bf16[2,256,128]{2,1,0:T(8,128)(2,1)S(1)}, u32[]{:S(2)}, u32[]{:S(2)}) collective-permute-start(bf16[2,256,128]{2,1,0:T(8,128)(2,1)S(1)} %get-tuple-element.36.refs_0_), channel_id=1, source_target_pairs={{4,8},{8,4},{12,16},{16,12},{20,24},{24,20},{5,9},{9,5},{13,17},{1... | collective-permute-start | bytes 393224 | tf_op jit(solution)/shard_map/ppermute | solution.py:213
  12.1 0.0 collective-permute-done.3.refs_4_
  12.1 0.3 collective-permute-done.4.refs_5_
  12.4 0.6 %join_keys.3 = (bf16[2,512,128]{2,1,0:T(8,128)(2,1)S(1)}, bf16[2,256,128]{2,1,0:T(8,128)(2,1)S(1)}) custom-call(bf16[2,256,128]{2,1,0:T(8,128)(2,1)S(1)} %get-tuple-element.36.refs_0_, s32[5]{0:T(128)S(1)} %stack.27.refs_0_.refs_1_, bf16[2,2,128,128]{3,2,1,0:T(8,128)(2,1)S(1)} %get-tuple-element.31.refs_0_.refs_2_, ...), custom_call_target="tpu_custom_call" | custom-call | tf_op jit(solution)/shard_map/join_keys/pallas_call | solution.py:33
  13.0 4.3 %collective-permute-start.6 = (bf16[2,256,128]{2,1,0:T(8,128)(2,1)S(1)}, bf16[2,256,128]{2,1,0:T(8,128)(2,1)S(1)}, u32[]{:S(2)}, u32[]{:S(2)}) collective-permute-start(bf16[2,256,128]{2,1,0:T(8,128)(2,1)S(1)} %get-tuple-element.39.refs_0_), channel_id=1, source_target_pairs={{0,4},{4,0},{8,12},{12,8},{16,20},{20,16},{24,28},{28,24},{1,5},{5... | collective-permute-start | bytes 393224 | tf_op jit(solution)/shard_map/ppermute | solution.py:214
  17.2 0.0 copy-done.1
  17.2 2.6 %late_blocks.2 = (bf16[256,1024]{1,0:T(8,128)(2,1)S(1)}, f32[2,512,128]{2,1,0:T(8,128)S(1)}) custom-call(bf16[2,256,128]{2,1,0:T(8,128)(2,1)S(1)} %get-tuple-element.39.refs_0_, s32[5]{0:T(128)S(1)} %stack.27.refs_0_.refs_1_, s32[64]{0:T(128)S(1)} %copy-done.1, bf16[1,2,512,1024]{3,2,1,0:T(8,128)(2,1)S(1)} %get-tuple-element.32.refs_0_.refs_3_, ...), custom_call_target="tpu_custom_call" | custom-call | flops 805306368 | tf_op jit(solution)/shard_map/late_blocks/pallas_call | solution.py:33
  19.8 0.0 collective-permute-done.5.refs_7_
  19.8 2.8 %early_blocks.2 = (bf16[256,1024]{1,0:T(8,128)(2,1)S(1)}, f32[2,256,128]{2,1,0:T(8,128)S(1)}, bf16[2,256,128]{2,1,0:T(8,128)(2,1)S(1)}) custom-call(f32[2,512,128]{2,1,0:T(8,128)S(1)} %get-tuple-element.42.refs_0_.refs_1_, s32[5]{0:T(128)S(1)} %stack.27.refs_0_.refs_1_, s32[64]{0:T(128)S(1)} %copy-done.1, ...), custom_call_target="tpu_custom_call" | custom-call | flops 805306368 | tf_op jit(solution)/shard_map/early_blocks/pallas_call | solution.py:33
  22.7 0.7 %collective-permute-start.7 = (bf16[2,256,128]{2,1,0:T(8,128)(2,1)S(1)}, bf16[2,256,128]{2,1,0:T(8,128)(2,1)S(1)}, u32[]{:S(2)}, u32[]{:S(2)}) collective-permute-start(bf16[2,256,128]{2,1,0:T(8,128)(2,1)S(1)} %get-tuple-element.44.refs_0_.refs_8_), channel_id=1, source_target_pairs={{4,8},{8,4},{12,16},{16,12},{20,24},{24,20},{5,9},{9,5},{13,17},{1... | collective-permute-start | bytes 393224 | tf_op jit(solution)/shard_map/ppermute | solution.py:213
  23.3 0.0 collective-permute-done.6.refs_7_
  23.3 3.1 %early_blocks.3 = (bf16[256,1024]{1,0:T(8,128)(2,1)S(1)}, f32[2,256,128]{2,1,0:T(8,128)S(1)}, bf16[2,256,128]{2,1,0:T(8,128)(2,1)S(1)}) custom-call(bf16[2,256,128]{2,1,0:T(8,128)(2,1)S(1)} %get-tuple-element.44.refs_0_.refs_8_, s32[5]{0:T(128)S(1)} %stack.27.refs_0_.refs_1_, s32[64]{0:T(128)S(1)} %copy-done.1, ...), custom_call_target="tpu_custom_call" | custom-call | flops 805306368 | tf_op jit(solution)/shard_map/early_blocks/pallas_call | solution.py:33
  26.5 5.8 %collective-permute-start.8 = (bf16[2,256,128]{2,1,0:T(8,128)(2,1)S(1)}, bf16[2,256,128]{2,1,0:T(8,128)(2,1)S(1)}, u32[]{:S(2)}, u32[]{:S(2)}) collective-permute-start(bf16[2,256,128]{2,1,0:T(8,128)(2,1)S(1)} %get-tuple-element.48.refs_0_.refs_4_), channel_id=1, source_target_pairs={{0,4},{4,0},{8,12},{12,8},{16,20},{20,16},{24,28},{28,24},{1,5},{5... | collective-permute-start | bytes 393224 | tf_op jit(solution)/shard_map/ppermute | solution.py:214
  32.2 2.8 %late_blocks.3 = (bf16[256,1024]{1,0:T(8,128)(2,1)S(1)}, f32[2,512,128]{2,1,0:T(8,128)S(1)}) custom-call(bf16[2,256,128]{2,1,0:T(8,128)(2,1)S(1)} %get-tuple-element.48.refs_0_.refs_4_, s32[5]{0:T(128)S(1)} %stack.27.refs_0_.refs_1_, s32[64]{0:T(128)S(1)} %copy-done.1, bf16[1,2,512,1024]{3,2,1,0:T(8,128)(2,1)S(1)} %get-tuple-element.32.refs_0_.refs_3_, ...), custom_call_target="tpu_custom_call" | custom-call | flops 805306368 | tf_op jit(solution)/shard_map/late_blocks/pallas_call | solution.py:33
  35.0 0.0 collective-permute-done.7.refs_3_
  35.0 0.1 collective-permute-done.8.refs_7_
  35.2 0.7 %pack_grads.1 = (bf16[2,2,128,128]{3,2,1,0:T(8,128)(2,1)S(1)}, bf16[2,2,128,128]{3,2,1,0:T(8,128)(2,1)S(1)}, bf16[2,2,128,128]{3,2,1,0:T(8,128)(2,1)S(1)}, bf16[2,2,128,128]{3,2,1,0:T(8,128)(2,1)S(1)}) custom-call(s32[5]{0:T(128)S(1)} %stack.27.refs_0_.refs_1_, f32[2,512,128]{2,1,0:T(8,128)S(1)} %get-tuple-element.42.refs_0_.refs_1_, ...), custom_call_target="tpu_custom_call" | custom-call | tf_op jit(solution)/shard_map/pack_grads/pallas_call | solution.py:33
  35.9 0.1 collective-permute-start.9
  36.0 1.6 %collective-permute-start.10 = (bf16[2,2,128,128]{3,2,1,0:T(8,128)(2,1)S(1)}, bf16[2,2,128,128]{3,2,1,0:T(8,128)(2,1)S(1)}, u32[]{:S(2)}, u32[]{:S(2)}) collective-permute-start(bf16[2,2,128,128]{3,2,1,0:T(8,128)(2,1)S(1)} %get-tuple-element.55), channel_id=1, source_target_pairs={{0,2},{1,3},{2,0},{3,1},{4,6},{5,7},{6,4},{7,5},{8,10},{9,11},{10,... | collective-permute-start | bytes 393224 | tf_op jit(solution)/shard_map/ppermute | solution.py:210
  37.5 0.3 collective-permute-start.11
  37.8 1.9 %store_queries.1 = bf16[1,2,512,1024]{3,2,1,0:T(8,128)(2,1)} custom-call(s32[5]{0:T(128)S(1)} %stack.27.refs_0_.refs_1_, bf16[256,1024]{1,0:T(8,128)(2,1)S(1)} %get-tuple-element.45.refs_1_, bf16[256,1024]{1,0:T(8,128)(2,1)S(1)} %get-tuple-element.46.refs_2_, bf16[256,1024]{1,0:T(8,128)(2,1)S(1)} %get-tuple-element.47.refs_3_, ...), custom_call_target="tpu_custom_call" | custom-call | tf_op jit(solution)/shard_map/store_queries/pallas_call | solution.py:33
  39.7 0.0 collective-permute-done.9.refs_2_
  39.7 2.6 %collective-permute-done.10.refs_3_ = bf16[2,2,128,128]{3,2,1,0:T(8,128)(2,1)S(1)} collective-permute-done((bf16[2,2,128,128]{3,2,1,0:T(8,128)(2,1)S(1)}, bf16[2,2,128,128]{3,2,1,0:T(8,128)(2,1)S(1)}, u32[]{:S(2)}, u32[]{:S(2)}) %collective-permute-start.10) | collective-permute-done | bytes 131104 | tf_op jit(solution)/shard_map/ppermute | solution.py:210
  42.3 1.9 %collective-permute-done.11.refs_4_ = bf16[2,2,128,128]{3,2,1,0:T(8,128)(2,1)S(1)} collective-permute-done((bf16[2,2,128,128]{3,2,1,0:T(8,128)(2,1)S(1)}, bf16[2,2,128,128]{3,2,1,0:T(8,128)(2,1)S(1)}, u32[]{:S(2)}, u32[]{:S(2)}) %collective-permute-start.11) | collective-permute-done | bytes 131104 | tf_op jit(solution)/shard_map/ppermute | solution.py:210
  44.2 1.5 %join_grads.1 = (bf16[1,2,128,512]{3,2,1,0:T(8,128)(2,1)}, bf16[1,2,128,512]{3,2,1,0:T(8,128)(2,1)}) custom-call(s32[5]{0:T(128)S(1)} %stack.27.refs_0_.refs_1_, bf16[2,2,128,128]{3,2,1,0:T(8,128)(2,1)S(1)} %get-tuple-element.53.refs_1_, bf16[2,2,128,128]{3,2,1,0:T(8,128)(2,1)S(1)} %collective-permute-done.9.refs_2_, ...), custom_call_target="tpu_custom_call" | custom-call | tf_op jit(solution)/shard_map/join_grads/pallas_call | solution.py:33
Async XLA Ops:
  2.4 8.4 %collective-permute-start = (bf16[2,2,128,128]{3,2,1,0:T(8,128)(2,1)S(1)}, bf16[2,2,128,128]{3,2,1,0:T(8,128)(2,1)S(1)}, u32[]{:S(2)}, u32[]{:S(2)}) collective-permute-start(bf16[2,2,128,128]{3,2,1,0:T(8,128)(2,1)S(1)} %get-tuple-element.33), channel_id=1, source_target_pairs={{0,1},{1,0},{2,3},{3,2},{4,5},{5,4},{6,7},{7,6},{8,9},{9,8},{10,11... | collective-permute-start | bytes 393224 | tf_op jit(solution)/shard_map/ppermute | solution.py:210
  3.0 7.8 %collective-permute-start.1 = (bf16[2,128,128]{2,1,0:T(8,128)(2,1)S(1)}, bf16[2,128,128]{2,1,0:T(8,128)(2,1)S(1)}, u32[]{:S(2)}, u32[]{:S(2)}) collective-permute-start(bf16[2,128,128]{2,1,0:T(8,128)(2,1)S(1)} %get-tuple-element.34), channel_id=1, source_target_pairs={{0,2},{1,3},{2,0},{3,1},{4,6},{5,7},{6,4},{7,5},{8,10},{9,11},{10,... | collective-permute-start | bytes 196616 | tf_op jit(solution)/shard_map/ppermute | solution.py:210
  5.5 5.3 %collective-permute-start.2 = (bf16[2,128,128]{2,1,0:T(8,128)(2,1)S(1)}, bf16[2,128,128]{2,1,0:T(8,128)(2,1)S(1)}, u32[]{:S(2)}, u32[]{:S(2)}) collective-permute-start(bf16[2,128,128]{2,1,0:T(8,128)(2,1)S(1)} %get-tuple-element.35), channel_id=1, source_target_pairs={{0,3},{1,2},{2,1},{3,0},{4,7},{5,6},{6,5},{7,4},{8,11},{9,10},{10,... | collective-permute-start | bytes 196616 | tf_op jit(solution)/shard_map/ppermute | solution.py:210
  5.6 6.5 %collective-permute-start.3 = (bf16[2,128,128]{2,1,0:T(8,128)(2,1)S(1)}, bf16[2,128,128]{2,1,0:T(8,128)(2,1)S(1)}, u32[]{:S(2)}, u32[]{:S(2)}) collective-permute-start(bf16[2,128,128]{2,1,0:T(8,128)(2,1)S(1)} %get-tuple-element.37), channel_id=1, source_target_pairs={{0,2},{1,3},{2,0},{3,1},{4,6},{5,7},{6,4},{7,5},{8,10},{9,11},{10,... | collective-permute-start | bytes 196616 | tf_op jit(solution)/shard_map/ppermute | solution.py:210
  7.3 5.0 %collective-permute-start.4 = (bf16[2,128,128]{2,1,0:T(8,128)(2,1)S(1)}, bf16[2,128,128]{2,1,0:T(8,128)(2,1)S(1)}, u32[]{:S(2)}, u32[]{:S(2)}) collective-permute-start(bf16[2,128,128]{2,1,0:T(8,128)(2,1)S(1)} %get-tuple-element.38), channel_id=1, source_target_pairs={{0,3},{1,2},{2,1},{3,0},{4,7},{5,6},{6,5},{7,4},{8,11},{9,10},{10,... | collective-permute-start | bytes 196616 | tf_op jit(solution)/shard_map/ppermute | solution.py:210
  7.3 0.7 %copy-start = (s32[64]{0:T(128)S(1)}, s32[64]{0:T(128)}, u32[]{:S(2)}) copy-start(s32[64]{0:T(128)} %refs_2_.11) | copy-start | bytes 772
  10.8 6.4 %copy-start.1 = (s32[64]{0:T(128)S(1)}, s32[64]{0:T(128)}, u32[]{:S(2)}) copy-start(s32[64]{0:T(128)} %refs_2_.11) | copy-start | bytes 772
  11.4 8.4 %collective-permute-start.5 = (bf16[2,256,128]{2,1,0:T(8,128)(2,1)S(1)}, bf16[2,256,128]{2,1,0:T(8,128)(2,1)S(1)}, u32[]{:S(2)}, u32[]{:S(2)}) collective-permute-start(bf16[2,256,128]{2,1,0:T(8,128)(2,1)S(1)} %get-tuple-element.36.refs_0_), channel_id=1, source_target_pairs={{4,8},{8,4},{12,16},{16,12},{20,24},{24,20},{5,9},{9,5},{13,17},{1... | collective-permute-start | bytes 393224 | tf_op jit(solution)/shard_map/ppermute | solution.py:213
  13.0 10.4 %collective-permute-start.6 = (bf16[2,256,128]{2,1,0:T(8,128)(2,1)S(1)}, bf16[2,256,128]{2,1,0:T(8,128)(2,1)S(1)}, u32[]{:S(2)}, u32[]{:S(2)}) collective-permute-start(bf16[2,256,128]{2,1,0:T(8,128)(2,1)S(1)} %get-tuple-element.39.refs_0_), channel_id=1, source_target_pairs={{0,4},{4,0},{8,12},{12,8},{16,20},{20,16},{24,28},{28,24},{1,5},{5... | collective-permute-start | bytes 393224 | tf_op jit(solution)/shard_map/ppermute | solution.py:214
  22.7 12.4 %collective-permute-start.7 = (bf16[2,256,128]{2,1,0:T(8,128)(2,1)S(1)}, bf16[2,256,128]{2,1,0:T(8,128)(2,1)S(1)}, u32[]{:S(2)}, u32[]{:S(2)}) collective-permute-start(bf16[2,256,128]{2,1,0:T(8,128)(2,1)S(1)} %get-tuple-element.44.refs_0_.refs_8_), channel_id=1, source_target_pairs={{4,8},{8,4},{12,16},{16,12},{20,24},{24,20},{5,9},{9,5},{13,17},{1... | collective-permute-start | bytes 393224 | tf_op jit(solution)/shard_map/ppermute | solution.py:213
  26.5 8.7 %collective-permute-start.8 = (bf16[2,256,128]{2,1,0:T(8,128)(2,1)S(1)}, bf16[2,256,128]{2,1,0:T(8,128)(2,1)S(1)}, u32[]{:S(2)}, u32[]{:S(2)}) collective-permute-start(bf16[2,256,128]{2,1,0:T(8,128)(2,1)S(1)} %get-tuple-element.48.refs_0_.refs_4_), channel_id=1, source_target_pairs={{0,4},{4,0},{8,12},{12,8},{16,20},{20,16},{24,28},{28,24},{1,5},{5... | collective-permute-start | bytes 393224 | tf_op jit(solution)/shard_map/ppermute | solution.py:214
  35.9 3.8 %collective-permute-start.9 = (bf16[2,2,128,128]{3,2,1,0:T(8,128)(2,1)S(1)}, bf16[2,2,128,128]{3,2,1,0:T(8,128)(2,1)S(1)}, u32[]{:S(2)}, u32[]{:S(2)}) collective-permute-start(bf16[2,2,128,128]{3,2,1,0:T(8,128)(2,1)S(1)} %get-tuple-element.54), channel_id=1, source_target_pairs={{0,1},{1,0},{2,3},{3,2},{4,5},{5,4},{6,7},{7,6},{8,9},{9,8},{10,11... | collective-permute-start | bytes 393224 | tf_op jit(solution)/shard_map/ppermute | solution.py:210
  36.0 6.4 %collective-permute-start.10 = (bf16[2,2,128,128]{3,2,1,0:T(8,128)(2,1)S(1)}, bf16[2,2,128,128]{3,2,1,0:T(8,128)(2,1)S(1)}, u32[]{:S(2)}, u32[]{:S(2)}) collective-permute-start(bf16[2,2,128,128]{3,2,1,0:T(8,128)(2,1)S(1)} %get-tuple-element.55), channel_id=1, source_target_pairs={{0,2},{1,3},{2,0},{3,1},{4,6},{5,7},{6,4},{7,5},{8,10},{9,11},{10,... | collective-permute-start | bytes 393224 | tf_op jit(solution)/shard_map/ppermute | solution.py:210
  37.5 6.7 %collective-permute-start.11 = (bf16[2,2,128,128]{3,2,1,0:T(8,128)(2,1)S(1)}, bf16[2,2,128,128]{3,2,1,0:T(8,128)(2,1)S(1)}, u32[]{:S(2)}, u32[]{:S(2)}) collective-permute-start(bf16[2,2,128,128]{3,2,1,0:T(8,128)(2,1)S(1)} %get-tuple-element.56), channel_id=1, source_target_pairs={{0,3},{1,2},{2,1},{3,0},{4,7},{5,6},{6,5},{7,4},{8,11},{9,10},{10,... | collective-permute-start | bytes 393224 | tf_op jit(solution)/shard_map/ppermute | solution.py:210
